TPU v7x, 256 devices: a whole 4x4x8 slice. The times are simulated.
256 devices in a mesh: side: 2 (over z_hi), fin: 4 (over x), fhid: 32 (over y, z_lo, core).
Axes of the slice: x: 4, y: 4, z: 8 (z_hi: 2, z_lo: 4; z = z_hi * 4 + z_lo), core: 2. Of those that a mesh axis runs over, the one named last changes fastest.
Arguments:
- queries: bfloat16 [256, 16384], P(('fin', 'fhid')), may hold values from -112 to 112
- new_entries: bfloat16 [256, 2048], P(('fin', 'fhid')), may hold values from -4 to 4
- cached_entries: bfloat16 [2, 256, 256, 2048], P('side', ('fin', 'fhid')), may hold values from -4 to 4
- lengths: int32 [256], P(('fin', 'fhid')), may hold values from 1 to 256, as said below
- residual: bfloat16 [256, 16384], P(('fin', 'fhid')), may hold values from -60 to 60
- norm_gain: bfloat16 [16384], P('fin'), may hold values from 0.099609375 to 1.8984375
- out_weight: bfloat16 [2, 16384, 16384], P('side', 'fhid', 'fin'), may hold values from -0.1875 to 0.1875
- gate_weight: bfloat16 [2, 16384, 8192], P('side', 'fin', 'fhid'), may hold values from -0.046875 to 0.046875
- up_weight: bfloat16 [2, 16384, 8192], P('side', 'fin', 'fhid'), may hold values from -0.046875 to 0.046875
- down_weight: bfloat16 [2, 8192, 16384], P('side', 'fhid', 'fin'), may hold values from -0.125 to 0.125
Outputs:
- next_hidden: bfloat16 [256, 16384], P(('fin', 'fhid'))
Inputs may be any that keep to these rules, and one draw needn't show every extreme that they name: `lengths`: every row has at least one and at most 256 cached positions in use; in every draw some rows use all 256.
All inputs are finite; a program needn't handle non-finite values.
Results may differ from a plain program's by a relative error of at most 0.011.
Values may be sent and summed in bfloat16 or wider, within the bound.
A program may use at most 128 MiB of HBM per device.

v0:
```python
import math

import jax
import jax.numpy as jnp
from jax import lax
from jax.sharding import PartitionSpec as P

D = 16384
HD = 128


def passed_along(block, axis, distance):
    devices = range(lax.axis_size(axis))
    route = [(i - distance, i) for i in devices if i - distance in devices]
    return lax.ppermute(block, axis, route)


def spread(block, axis, holder):
    block = jnp.where(lax.axis_index(axis) == holder, block, jnp.zeros_like(block))
    return lax.psum(block, axis)


def attend(queries, new_entries, cached, lengths):
    row_count = queries.shape[0]
    positions = cached.shape[1]
    key_width = cached.shape[2] // 2
    heads_kv = key_width // HD
    per_group = queries.shape[1] // key_width
    score_scale = 1.0 / math.sqrt(HD)
    cached_keys = cached[:, :, :key_width].reshape(row_count, positions, heads_kv, HD)
    cached_values = cached[:, :, key_width:].reshape(row_count, positions, heads_kv, HD)
    heads = queries.reshape(row_count, heads_kv, per_group, HD)
    new_key = new_entries[:, :key_width].reshape(row_count, heads_kv, HD)
    new_value = new_entries[:, key_width:].reshape(row_count, heads_kv, HD)
    scores = (
        jnp.einsum("rgqd,rlgd->rgql", heads, cached_keys, preferred_element_type=jnp.float32)
        * score_scale
    )
    own_score = (
        jnp.einsum("rgqd,rgd->rgq", heads, new_key, preferred_element_type=jnp.float32)
        * score_scale
    )
    valid = jnp.arange(positions)[None, :] < lengths[:, None]
    scores = jnp.where(valid[:, None, None, :], scores, jnp.float32(-1e30))
    row_top = jnp.maximum(jnp.max(scores, axis=-1), own_score)
    expo = jnp.exp(scores - row_top[..., None])
    own_exp = jnp.exp(own_score - row_top)
    denominator = jnp.sum(expo, axis=-1) + own_exp
    weights = (expo / denominator[..., None]).astype(jnp.bfloat16)
    own_weight = (own_exp / denominator).astype(jnp.bfloat16)
    mixed = jnp.einsum(
        "rgql,rlgd->rgqd", weights, cached_values, preferred_element_type=jnp.float32
    )
    mixed = (
        mixed
        + own_weight.astype(jnp.float32)[..., None] * new_value.astype(jnp.float32)[:, :, None, :]
    )
    return mixed.reshape(row_count, -1).astype(jnp.bfloat16)


def normalize(stream, norm_gain, total_square):
    stream_wide = stream.astype(jnp.float32)
    scaled = stream_wide * lax.rsqrt(total_square[:, None] / D + 1e-05)
    return (scaled * norm_gain.astype(jnp.float32)).astype(jnp.bfloat16)


def layer(
    queries,
    new_entries,
    cached,
    lengths,
    residual,
    norm_gain,
    out_block,
    gate_block,
    up_block,
    down_block,
):
    mixed = attend(queries, new_entries, cached, lengths)
    arrived = passed_along(mixed, "side", 1)
    grouped = lax.all_gather(arrived, "fin", axis=0, tiled=True)
    head_rows = lax.all_to_all(grouped, "fhid", split_axis=1, concat_axis=0, tiled=True)
    resid_block = lax.all_to_all(residual, "fin", split_axis=1, concat_axis=0, tiled=True)
    block_rows = resid_block.shape[0]
    partial_value = jnp.dot(head_rows, out_block, preferred_element_type=jnp.float32)
    projected = lax.psum(partial_value, "fhid")
    resid_all = lax.all_gather(resid_block, "fhid", axis=0, tiled=True)
    stream_all = (resid_all.astype(jnp.float32) + projected).astype(jnp.bfloat16)
    stream_wide = stream_all.astype(jnp.float32)
    total_square = lax.psum(jnp.sum(stream_wide * stream_wide, axis=1), "fin")
    normed = normalize(stream_all, norm_gain, total_square)
    paired = jnp.concatenate(
        [
            jnp.dot(normed, gate_block, preferred_element_type=jnp.float32),
            jnp.dot(normed, up_block, preferred_element_type=jnp.float32),
        ],
        axis=1,
    )
    stream = lax.dynamic_slice_in_dim(
        stream_all, lax.axis_index("fhid") * block_rows, block_rows, 0
    )
    paired = lax.psum(paired, "fin")
    hidden_width = gate_block.shape[1]
    hidden = (jax.nn.silu(paired[:, :hidden_width]) * paired[:, hidden_width:]).astype(jnp.bfloat16)
    lowered = lax.psum_scatter(
        jnp.dot(hidden, down_block, preferred_element_type=jnp.float32),
        "fhid",
        scatter_dimension=0,
        tiled=True,
    )
    updated = (stream.astype(jnp.float32) + lowered).astype(jnp.bfloat16)
    row_major = lax.all_to_all(updated, "fin", split_axis=0, concat_axis=1, tiled=True)
    return spread(row_major, "side", 1)


def on_device(
    queries,
    new_entries,
    cached_entries,
    lengths,
    residual,
    norm_gain,
    out_weight,
    gate_weight,
    up_weight,
    down_weight,
):
    portions = 1
    stride = queries.shape[0] // portions
    results = layer(
        queries,
        new_entries,
        cached_entries[0, 0:stride],
        lengths,
        residual,
        norm_gain,
        out_weight[0],
        gate_weight[0],
        up_weight[0],
        down_weight[0],
    )
    return results


def solution(mesh):
    placed = (
        P(("fin", "fhid"), None),
        P(("fin", "fhid"), None),
        P("side", ("fin", "fhid"), None, None),
        P(("fin", "fhid")),
        P(("fin", "fhid"), None),
        P("fin"),
        P("side", "fhid", "fin"),
        P("side", "fin", "fhid"),
        P("side", "fin", "fhid"),
        P("side", "fhid", "fin"),
    )
    return jax.shard_map(
        on_device, mesh=mesh, in_specs=placed, out_specs=P(("fin", "fhid"), None), check_vma=False
    )
```

profile of v0, /device:TPU:1, one launch (start us, length us, event | category | flops | bytes accessed | tf_op | source)
XLA Modules:
  0.0 649.8 jit_solution(7476202331253191338)
XLA Ops:
  6.5 9.4 %all_to_all.51 = bf16[2,4,4096]{2,0,1:T(2,128)(2,1)S(1)} all-to-all(bf16[2,4,4096]{2,0,1:T(2,128)(2,1)} %bitcast.54), channel_id=1, replica_groups=mesh['side'=2,'fin'=4,'fhid'=32] {'fin'}, dimensions={1} | all-to-all | bytes 131072 | tf_op jit(solution)/shard_map/all_to_all | solution.py:83
  16.8 3.9 copy.25
  21.0 1.7 fusion.25
  23.8 8.8 %collective-permute-start = (bf16[2,16384]{1,0:T(2,128)(2,1)S(1)}, bf16[2,16384]{1,0:T(2,128)(2,1)S(1)}, u32[]{:S(2)}, u32[]{:S(2)}) collective-permute-start(bf16[2,16384]{1,0:T(2,128)(2,1)S(1)} %bitcast.57), channel_id=1, source_target_pairs={{0,128},{1,129},{2,130},{3,131},{4,132},{5,133},{6,134},{7,135},{8... | collective-permute-start | bytes 196616 | tf_op jit(solution)/shard_map/ppermute | solution.py:15
  32.6 1.3 collective-permute-done
  33.9 9.4 %all-gather = bf16[4,2,16384]{2,1,0:T(2,128)(2,1)S(1)} all-gather(bf16[1,2,16384]{2,1,0:T(2,128)(2,1)S(1)} %bitcast.53), channel_id=1, replica_groups=mesh['side'=2,'fin'=4,'fhid'=32] {'fin'}, dimensions={0}, use_global_device_ids=true | all-gather | bytes 327680 | tf_op jit(solution)/shard_map/all_gather | solution.py:81
  43.6 23.5 %all_to_all.52 = bf16[8,32,512]{2,0,1:T(8,128)(2,1)S(1)} all-to-all(bf16[8,32,512]{2,0,1:T(8,128)(2,1)S(1)} %copy.28), channel_id=1, replica_groups=mesh['side'=2,'fin'=4,'fhid'=32] {'fhid'}, dimensions={1} | all-to-all | bytes 524288 | tf_op jit(solution)/shard_map/all_to_all | solution.py:82
  67.1 5.5 fusion.3
  73.2 8.3 %all-gather.3.cloned.1.call-done = bf16[256,4096]{1,0:T(8,128)(2,1)} async-done(((bf16[8,4096]{1,0:T(8,128)(2,1)}), bf16[256,4096]{1,0:T(8,128)(2,1)}) %all-gather.3.cloned.1.call-update) | async-done | bytes 2097168 | tf_op jit(solution)/shard_map/all_gather | solution.py:87
  81.6 292.9 %all-reduce.4.cloned.1.call-done = f32[256,4096]{1,0:T(8,128)} async-done(((f32[256,4096]{1,0:T(8,128)}), f32[256,4096]{1,0:T(8,128)}) %all-reduce.4.cloned.1.call-update) | async-done | bytes 4194320 | tf_op jit(solution)/shard_map/psum | solution.py:86
  374.5 5.0 fusion
  379.5 8.8 %psum.29 = f32[256]{0:T(256)S(1)} all-reduce(f32[256]{0:T(256)S(1)} %get-tuple-element.5), channel_id=1, replica_groups=mesh['side'=2,'fin'=4,'fhid'=32] {'fin'}, use_global_device_ids=true, to_apply=%region_4.5 | all-reduce | flops 256 | bytes 2048 | tf_op jit(solution)/shard_map/psum | solution.py:90
  388.3 3.5 fusion.9
  391.9 1.2 fusion.7
  393.0 0.8 pad_maximum_fusion
  393.9 44.9 %all-reduce.6.cloned.1.call-done = f32[256,512]{0,1:T(8,128)} async-done(((f32[256,512]{0,1:T(8,128)}), f32[256,512]{0,1:T(8,128)}) %all-reduce.6.cloned.1.call-update) | async-done | bytes 524304 | tf_op jit(solution)/shard_map/psum | solution.py:102
  438.9 3.7 fusion.5
  442.7 150.9 %reduce-scatter.2.cloned.1.call-done = f32[8,4096]{1,0:T(8,128)} async-done(((f32[256,4096]{1,0:T(8,128)}), f32[8,4096]{1,0:T(8,128)}) %reduce-scatter.2.cloned.1.call-update) | async-done | bytes 131088 | tf_op jit(solution)/shard_map/reduce_scatter | solution.py:105
  593.6 0.9 add_convert_fusion.1
  594.5 0.7 all_to_all.46
  595.2 3.7 all-to-all-start.2
  598.9 4.5 all-to-all-done.2
  604.1 37.7 %all-reduce.8.cloned.1.call-done = bf16[2,16384]{1,0:T(2,128)(2,1)} async-done(((bf16[2,16384]{1,0:T(2,128)(2,1)}), bf16[2,16384]{1,0:T(2,128)(2,1)}) %all-reduce.8.cloned.1.call-update) | async-done | bytes 65552 | tf_op jit(solution)/shard_map/psum | solution.py:20
  641.8 1.5 copy.44
  (42 shorter events, 3.9 us)
Async XLA Ops:
  6.5 432.3 %copy-start = (bf16[1,256,4096]{2,1,0:T(8,128)(2,1)S(1)}, bf16[1,256,4096]{2,1,0:T(8,128)(2,1)}, u32[]{:S(2)}) copy-start(bf16[1,256,4096]{2,1,0:T(8,128)(2,1)} %param.19) | copy-start | bytes 6291460
  6.5 75.0 %all-gather.3.cloned.1.call-start = ((), (), s32[]{:S(2)}) async-start(), calls=%async_computation.4 | async-start | bytes 2162688 | tf_op jit(solution)/shard_map/all_gather | solution.py:87
  16.7 4.0 copy-start.2
  16.7 4.0 copy-start.4
  16.7 4.1 copy-start.6
  16.7 357.8 %all-reduce.4.cloned.1.call-start = ((), (), s32[]{:S(2)}) async-start(), calls=%async_computation.5 | async-start | bytes 8388608 | tf_op jit(solution)/shard_map/psum | solution.py:86
  23.8 10.1 %collective-permute-start = (bf16[2,16384]{1,0:T(2,128)(2,1)S(1)}, bf16[2,16384]{1,0:T(2,128)(2,1)S(1)}, u32[]{:S(2)}, u32[]{:S(2)}) collective-permute-start(bf16[2,16384]{1,0:T(2,128)(2,1)S(1)} %bitcast.57), channel_id=1, source_target_pairs={{0,128},{1,129},{2,130},{3,131},{4,132},{5,133},{6,134},{7,135},{8... | collective-permute-start | bytes 196616 | tf_op jit(solution)/shard_map/ppermute | solution.py:15
  72.5 0.7 copy-start.3
  72.6 366.3 %all-reduce.6.cloned.1.call-start = ((), (), s32[]{:S(2)}) async-start(), calls=%async_computation.6 | async-start | bytes 1048576 | tf_op jit(solution)/shard_map/psum | solution.py:102
  388.3 3.5 copy-start.1
  388.3 3.5 copy-start.5
  393.9 199.7 %reduce-scatter.2.cloned.1.call-start = ((), (), s32[]{:S(2)}) async-start(), calls=%async_computation.7 | async-start | bytes 4325376 | tf_op jit(solution)/shard_map/reduce_scatter | solution.py:105
  595.2 8.2 %all-to-all-start.2 = ((bf16[4,2,4096]{2,1,0:T(2,128)(2,1)}), bf16[4,2,4096]{2,1,0:T(2,128)(2,1)S(1)}, u32[]{:S(2)}, u32[]{:S(2)}) async-start(bf16[4,2,4096]{2,1,0:T(2,128)(2,1)} %all_to_all.46), calls=%async_computation.3 | async-start | bytes 131072 | tf_op jit(solution)/shard_map/all_to_all | solution.py:112
  598.9 42.9 %all-reduce.8.cloned.1.call-start = ((), (), s32[]{:S(2)}) async-start(), calls=%async_computation.8 | async-start | bytes 131072 | tf_op jit(solution)/shard_map/psum | solution.py:20
Sparse Core Ops, SparseCore 0:
  16.8 64.7 all-gather.2
  84.2 290.2 all-reduce.3
  394.0 44.8 all-reduce.5
  442.8 150.7 reduce-scatter.1
  604.2 37.5 all-reduce.7
where the time goes:
time: 650 us
  waiting for transfers between devices  541 us (83%)
  blocking collectives  51.1 us (8%)
  matrix products  14.8 us (2%)
  between operations  13.3 us (2%)
  starting transfers between devices  12.6 us (2%)
  local copies, waits for them, and re-layouts  9.57 us (1%)
  other arithmetic  7.77 us (1%)
    psum x1, waiting for transfers between devices, layer(): projected = lax.psum(partial_value, 'fhid')  293 us
    reduce_scatter x1, waiting for transfers between devices, layer(): lax.psum_scatter(jnp.dot(hidden, down_block, preferred_element_type=jnp.f...  151 us
    psum x1, waiting for transfers between devices, layer(): paired = lax.psum(paired, 'fin')  44.9 us
    psum x1, waiting for transfers between devices, spread(): return lax.psum(block, axis)  37.7 us
    all_to_all x1, blocking collectives, layer(): lax.all_to_all(grouped, 'fhid', split_axis=1, concat_axis=0, tiled=True)  23.5 us
  transfers between devices with their start and end apart: 7, of which 7 were waited for; matrix products, arithmetic and copies ran while one was open for 2% of the time, Pallas kernels for 0%

commit v1 on v0

v1 whole, which is shorter than its diff:
```python
import functools
import math

import jax
import jax.numpy as jnp
from jax import lax
from jax.experimental import pallas as pl
from jax.experimental.pallas import tpu as pltpu
from jax.sharding import PartitionSpec as P

D = 16384
HD = 128
BF = jnp.bfloat16
F32 = jnp.float32
MESH = pl.DeviceIdType.MESH
ORDER = (2, 1, 3, 0)


def attend(queries, new_entries, cached, lengths):
    row_count = queries.shape[0]
    positions = cached.shape[1]
    key_width = cached.shape[2] // 2
    heads_kv = key_width // HD
    per_group = queries.shape[1] // key_width
    score_scale = 1.0 / math.sqrt(HD)
    cached_keys = cached[:, :, :key_width].reshape(row_count, positions, heads_kv, HD)
    cached_values = cached[:, :, key_width:].reshape(row_count, positions, heads_kv, HD)
    heads = queries.reshape(row_count, heads_kv, per_group, HD)
    new_key = new_entries[:, :key_width].reshape(row_count, heads_kv, HD)
    new_value = new_entries[:, key_width:].reshape(row_count, heads_kv, HD)
    scores = (
        jnp.einsum("rgqd,rlgd->rgql", heads, cached_keys, preferred_element_type=F32) * score_scale
    )
    own_score = (
        jnp.einsum("rgqd,rgd->rgq", heads, new_key, preferred_element_type=F32) * score_scale
    )
    valid = jnp.arange(positions)[None, :] < lengths[:, None]
    scores = jnp.where(valid[:, None, None, :], scores, jnp.float32(-1e30))
    row_top = jnp.maximum(jnp.max(scores, axis=-1), own_score)
    expo = jnp.exp(scores - row_top[..., None])
    own_exp = jnp.exp(own_score - row_top)
    denominator = jnp.sum(expo, axis=-1) + own_exp
    weights = (expo / denominator[..., None]).astype(BF)
    own_weight = (own_exp / denominator).astype(BF)
    mixed = jnp.einsum("rgql,rlgd->rgqd", weights, cached_values, preferred_element_type=F32)
    mixed = (
        mixed + own_weight.astype(F32)[..., None] * new_value.astype(F32)[:, :, None, :]
    )
    return mixed.reshape(row_count, -1).astype(BF)


def iota(shape, axis):
    return lax.broadcasted_iota(jnp.int32, shape, axis)


def selection(source):
    t = iota((256, 256), 0)
    return (iota((256, 256), 1) == source(t)).astype(F32).astype(BF)


def arrived(ref, sem):
    pltpu.make_async_copy(ref, ref, sem).wait()


def kernel(
    m1_src, res_src, gain, ow_hbm, gw_hbm, uw_hbm, dw_hbm, out,
    ow, gw, uw, dw, m1, m2s, m2, lhs, rin, resid, acc,
    own, cs, cr, q, ya, yb, yfm, yfp, zs, zin,
    sbuf, gu, ss, xs, xr, hid,
    own2, cs2, cr2, q2, ya2, yb2, yfm2, yfp2, zs2, zin2, fo, fb, fin_in,
    w_sem, m1_s, m1_r, m2_s, m2_r, rs_s, rs_r, xa_s, xa_r, c_s, c_r, y_s, y_r, z_s, z_r,
    az_s, ay_s, ac_s, ag_r, ac_r, xs_s, xs_r, xh_s, xh_r, c2_s, c2_r, y2_s, y2_r, z2_s, z2_r,
    f_s, f_r,
):
    side, f, h = lax.axis_index("side"), lax.axis_index("fin"), lax.axis_index("fhid")
    y, z, c = h // 8, (h // 2) % 4, h % 2
    yz = h // 2
    oc = 1 - c

    def at(s, ff, yy, zz, cc):
        return (s, ff, (yy * 4 + zz) * 2 + cc)

    def send(src, dst, ss_, rs_, dev):
        cp = pltpu.make_async_remote_copy(
            src_ref=src, dst_ref=dst, send_sem=ss_, recv_sem=rs_, device_id=dev, device_id_type=MESH
        )
        cp.start()
        return cp

    barrier = pltpu.get_barrier_semaphore()

    def greet(dev):
        pl.semaphore_signal(barrier, inc=1, device_id=dev, device_id_type=MESH)

    j = f * 2 + c

    @pl.when(side == 0)
    def _attention_side():
        for d in range(1, 8):
            jj = (j + d) % 8
            greet(at(0, jj // 2, y, z, jj % 2))
        for d in range(8):
            greet(at(1, d // 2, y, z, d % 2))
        pl.semaphore_wait(barrier, 23)
        copies = []
        for d in range(1, 8):
            jj = (j + d) % 8
            copies.append(
                send(m1_src.at[jj], m1.at[j], m1_s.at[d], m1_r.at[j], at(0, jj // 2, y, z, jj % 2))
            )
        m1[j] = m1_src[j]
        sel = selection(
            lambda t: (((t // 2) % 4 * 2 + (t // 8) % 2) * 2 + t % 2) * 16 + t // 16
        )
        for d in range(1, 8):
            jj = (j + d) % 8
            arrived(m1.at[jj], m1_r.at[jj])
        m2s[...] = jnp.dot(sel, m1[...].reshape(256, 128), preferred_element_type=F32).astype(BF)
        for b in range(16):
            copies.append(
                send(
                    m2s.at[pl.ds(b * 16, 16)],
                    m2.at[pl.ds(pl.multiple_of(yz * 16, 16), 16)],
                    m2_s.at[b],
                    m2_r.at[yz],
                    at(1, f, b // 4, b % 4, c),
                )
            )
        for cp in copies:
            cp.wait_send()
        for s in range(8):
            arrived(fin_in.at[s], f_r.at[s])
        out[...] = fin_in[...]

    @pl.when(side == 1)
    def _mlp_side():
        up, down = (y + 1) % 4, (y + 3) % 4
        dev_up, dev_down = at(1, f, up, z, c), at(1, f, down, z, c)
        dev_core = at(1, f, y, z, oc)
        for d in range(16):
            greet(at(0, f, d // 4, d % 4, c))
        for d in range(1, 8):
            jj = (j + d) % 8
            greet(at(1, jj // 2, y, z, jj % 2))
        for d in range(1, 4):
            greet(at(1, f, y, (z + d) % 4, c))
        greet(dev_up)
        greet(dev_down)
        weights = [
            pltpu.make_async_copy(a, b, w_sem.at[k])
            for k, (a, b) in enumerate(((ow_hbm, ow), (gw_hbm, gw), (uw_hbm, uw), (dw_hbm, dw)))
        ]
        for cp in weights:
            cp.start()
        pl.semaphore_wait(barrier, 20)
        copies = []

        for d in range(1, 4):
            ff = (f + d) % 4
            copies.append(
                send(res_src.at[ff], rin.at[f], rs_s.at[d], rs_r.at[f], at(1, ff, y, z, c))
            )
        rin[f] = res_src[f]
        for d in range(1, 4):
            ff = (f + d) % 4
            arrived(rin.at[ff], rs_r.at[ff])
        sel = selection(
            lambda t: (t // 2) % 4 * 64 + ((t % 2) * 16 + (t // 8) % 16) * 2 + t // 128
        )
        resid[...] = jnp.dot(sel, rin[...].reshape(256, 128), preferred_element_type=F32)
        gu[...] = jnp.zeros_like(gu)
        ss[...] = jnp.zeros_like(ss)

        for s in range(16):
            arrived(m2.at[pl.ds(s * 16, 16)], m2_r.at[s])
        for d in range(1, 4):
            ff = (f + d) % 4
            copies.append(send(m2, lhs.at[f], xa_s.at[d], xa_r.at[f], at(1, ff, y, z, c)))
        lhs[f] = m2[...]
        weights[0].wait()
        for d in range(1, 4):
            ff = (f + d) % 4
            arrived(lhs.at[ff], xa_r.at[ff])

        def project(g):
            yy = (y + ORDER[g]) % 4

            def chunk(k, carry):
                n = yy * 4 + k
                x = jnp.concatenate([lhs[0], lhs[1], lhs[2], lhs[3]], axis=1)
                w = ow[:, pl.ds(pl.multiple_of(n * 256, 256), 256)]
                acc[...] = jnp.dot(x, w, preferred_element_type=F32)
                r8 = pl.ds(pl.multiple_of(h * 8, 8), 8)
                lo = resid[pl.ds(pl.multiple_of(n * 8, 8), 8), :]
                hi = resid[pl.ds(pl.multiple_of(128 + n * 8, 8), 8), :]
                acc[r8, :] = acc[r8, :] + jnp.concatenate([lo, hi], axis=1)
                own[n] = acc[pl.ds(pl.multiple_of(c * 128, 128), 128), :]
                cs[n] = acc[pl.ds(pl.multiple_of(oc * 128, 128), 128), :].astype(BF)
                return carry

            lax.fori_loop(0, 4, chunk, 0)
            part = pl.ds(yy * 4, 4)
            copies.append(send(cs.at[part], cr.at[part], c_s.at[g], c_r.at[g], dev_core))

        def paired(g):
            yy = (y + ORDER[g]) % 4
            part = pl.ds(yy * 4, 4)
            arrived(cr.at[part], c_r.at[g])
            if g < 3:
                q[part] = (own[part] + cr[part].astype(F32)).astype(BF)
            first, second = pl.ds(yy * 4, 2), pl.ds(yy * 4 + 2, 2)
            a, b = pl.ds(0, 2), pl.ds(2, 2)
            if g == 0:
                copies.append(send(q.at[first], ya, y_s.at[0], y_r.at[0], dev_up))
                copies.append(send(q.at[second], yb, y_s.at[1], y_r.at[1], dev_down))
            if g == 1:
                copies.append(send(q.at[second], yfm.at[b], y_s.at[2], y_r.at[2], dev_up))
            if g == 2:
                copies.append(send(q.at[first], yfp.at[a], y_s.at[3], y_r.at[3], dev_down))

        project(0)
        project(1)
        paired(0)
        project(2)
        paired(1)
        project(3)
        paired(2)
        a, b = pl.ds(0, 2), pl.ds(2, 2)
        arrived(ya, y_r.at[0])
        first = pl.ds(up * 4, 2)
        q[first] = (q[first].astype(F32) + ya[...].astype(F32)).astype(BF)
        copies.append(send(q.at[first], yfm.at[a], y_s.at[4], y_r.at[4], dev_up))
        arrived(yb, y_r.at[1])
        second = pl.ds(down * 4 + 2, 2)
        q[second] = (q[second].astype(F32) + yb[...].astype(F32)).astype(BF)
        copies.append(send(q.at[second], yfp.at[b], y_s.at[5], y_r.at[5], dev_down))
        paired(3)
        arrived(yfm.at[b], y_r.at[2])
        arrived(yfp.at[a], y_r.at[3])
        arrived(yfm.at[a], y_r.at[4])
        arrived(yfp.at[b], y_r.at[5])

        def summed(k):
            n = y * 4 + k
            return own[n] + cr[n].astype(F32) + yfm[k].astype(F32) + yfp[k].astype(F32)

        for d in range(1, 4):
            zz = (z + d) % 4
            zs[zz] = summed(zz).astype(BF)
            copies.append(send(zs.at[zz], zin.at[z], z_s.at[d], z_r.at[z], at(1, f, y, zz, c)))
        total = summed(z)
        for d in range(1, 4):
            zz = (z + d) % 4
            arrived(zin.at[zz], z_r.at[zz])
            total = total + zin[zz].astype(F32)
        sbuf[yz, c] = total.astype(BF)

        def give(n, sem, slot, dev):
            copies.append(
                send(sbuf.at[n, c], sbuf.at[n, c], sem.at[slot], ag_r.at[n], dev)
            )

        def give_core(n):
            copies.append(
                send(sbuf.at[n, c], sbuf.at[n, c], ac_s.at[n], ac_r.at[n], dev_core)
            )

        def use(n):
            arrived(sbuf.at[n, oc], ac_r.at[n])
            x = sbuf[n].reshape(256, 256).astype(F32)
            sq = x * x
            ss[...] += sq[:, :128] + sq[:, 128:]
            xg = (x * gain[n]).astype(BF)
            rows = pl.ds(pl.multiple_of(n * 256, 256), 256)
            gu[:, :256] += jnp.dot(xg, gw[rows, :], preferred_element_type=F32)
            gu[:, 256:] += jnp.dot(xg, uw[rows, :], preferred_element_type=F32)

        for d in range(1, 4):
            zz = (z + d) % 4
            give(yz, az_s, d, at(1, f, y, zz, c))
        give(yz, ay_s, 0, dev_up)
        give(yz, ay_s, 1, dev_down)
        give_core(yz)
        for d in range(1, 4):
            n = y * 4 + (z + d) % 4
            arrived(sbuf.at[n, c], ag_r.at[n])
            give(n, ay_s, d * 2, dev_up)
            give(n, ay_s, d * 2 + 1, dev_down)
            give_core(n)
        weights[1].wait()
        weights[2].wait()
        use(yz)
        for d in range(4):
            n = down * 4 + (z + d) % 4
            arrived(sbuf.at[n, c], ag_r.at[n])
            if d % 2 == 0:
                give(n, ay_s, 8 + d, dev_up)
            give_core(n)
            n = up * 4 + (z + d) % 4
            arrived(sbuf.at[n, c], ag_r.at[n])
            if d % 2 == 1:
                give(n, ay_s, 8 + d, dev_down)
            give_core(n)
            if d > 0:
                use(y * 4 + (z + d) % 4)
        far = (y + 2) % 4
        for d in range(4):
            use(down * 4 + (z + d) % 4)
            use(up * 4 + (z + d) % 4)
            n = far * 4 + (z + d) % 4
            arrived(sbuf.at[n, c], ag_r.at[n])
            give_core(n)
        for d in range(4):
            use(far * 4 + (z + d) % 4)

        tot = jnp.sum(ss[...], axis=1, keepdims=True)
        top = tot.astype(BF).astype(F32)
        lanes = iota((256, 128), 1)
        xs[:, :, 512:] = jnp.where(lanes < 64, top, tot - top).astype(BF).reshape(4, 64, 128)
        xs[:, :, :512] = gu[...].astype(BF).reshape(4, 64, 512)
        for d in range(1, 4):
            ff = (f + d) % 4
            copies.append(send(xs.at[ff], xr.at[f], xs_s.at[d], xs_r.at[f], at(1, ff, y, z, c)))
        mine = pl.ds(pl.multiple_of(f * 64, 64), 64)
        both = gu[mine, :]
        square = xs[f][:, 512:].astype(F32)
        for d in range(1, 4):
            ff = (f + d) % 4
            arrived(xr.at[ff], xs_r.at[ff])
            both = both + xr[ff][:, :512].astype(F32)
            square = square + xr[ff][:, 512:].astype(F32)
        scale = lax.rsqrt((square[:, 0:1] + square[:, 64:65]) / D + 1e-05)
        gate = both[:, :256] * scale
        hid[mine, :] = (gate / (1.0 + jnp.exp(-gate)) * (both[:, 256:] * scale)).astype(BF)
        for d in range(1, 4):
            ff = (f + d) % 4
            copies.append(
                send(hid.at[mine], hid.at[mine], xh_s.at[d], xh_r.at[f], at(1, ff, y, z, c))
            )
        weights[3].wait()
        for d in range(1, 4):
            ff = (f + d) % 4
            arrived(hid.at[pl.ds(pl.multiple_of(ff * 64, 64), 64)], xh_r.at[ff])

        def lower(g):
            yy = (y + ORDER[g]) % 4

            def chunk(k, carry):
                x = hid[pl.ds(pl.multiple_of(yy * 64, 64), 64), :]
                to = pl.ds(pl.multiple_of(k * 512, 512), 512)
                w = dw[:, pl.ds(pl.multiple_of(oc * 2048 + k * 512, 512), 512)]
                cs2[yy, :, to] = jnp.dot(x, w, preferred_element_type=F32).astype(BF)
                w = dw[:, pl.ds(pl.multiple_of(c * 2048 + k * 512, 512), 512)]
                own2[yy, :, to] = jnp.dot(x, w, preferred_element_type=F32)
                return carry

            lax.fori_loop(0, 4, chunk, 0)
            copies.append(send(cs2.at[yy], cr2.at[yy], c2_s.at[g], c2_r.at[g], dev_core))

        a2, b2 = pl.ds(0, 32), pl.ds(32, 32)

        def paired2(g):
            yy = (y + ORDER[g]) % 4
            arrived(cr2.at[yy], c2_r.at[g])
            if g < 3:
                q2[yy] = (own2[yy] + cr2[yy].astype(F32)).astype(BF)
            if g == 0:
                copies.append(send(q2.at[yy, a2], ya2, y2_s.at[0], y2_r.at[0], dev_up))
                copies.append(send(q2.at[yy, b2], yb2, y2_s.at[1], y2_r.at[1], dev_down))
            if g == 1:
                copies.append(send(q2.at[yy, b2], yfm2.at[b2], y2_s.at[2], y2_r.at[2], dev_up))
            if g == 2:
                copies.append(send(q2.at[yy, a2], yfp2.at[a2], y2_s.at[3], y2_r.at[3], dev_down))

        lower(0)
        lower(1)
        paired2(0)
        lower(2)
        paired2(1)
        lower(3)
        paired2(2)
        arrived(ya2, y2_r.at[0])
        q2[up, a2] = (q2[up, a2].astype(F32) + ya2[...].astype(F32)).astype(BF)
        copies.append(send(q2.at[up, a2], yfm2.at[a2], y2_s.at[4], y2_r.at[4], dev_up))
        arrived(yb2, y2_r.at[1])
        q2[down, b2] = (q2[down, b2].astype(F32) + yb2[...].astype(F32)).astype(BF)
        copies.append(send(q2.at[down, b2], yfp2.at[b2], y2_s.at[5], y2_r.at[5], dev_down))
        paired2(3)
        arrived(yfm2.at[b2], y2_r.at[2])
        arrived(yfp2.at[a2], y2_r.at[3])
        arrived(yfm2.at[a2], y2_r.at[4])
        arrived(yfp2.at[b2], y2_r.at[5])

        def summed2(k):
            rows = pl.ds(pl.multiple_of(k * 16, 16), 16)
            return (
                own2[y, rows, :]
                + cr2[y, rows, :].astype(F32)
                + yfm2[rows, :].astype(F32)
                + yfp2[rows, :].astype(F32)
            )

        for d in range(1, 4):
            zz = (z + d) % 4
            zs2[zz] = summed2(zz).astype(BF)
            copies.append(
                send(zs2.at[zz], zin2.at[z], z2_s.at[d], z2_r.at[z], at(1, f, y, zz, c))
            )
        rows = pl.ds(pl.multiple_of((yz % 8) * 16, 16), 16)
        kept = [sbuf[c * 8 + k, y // 2, rows, :].astype(F32) for k in range(8)]
        total = summed2(z) + jnp.concatenate(kept, axis=1)
        for d in range(1, 4):
            zz = (z + d) % 4
            arrived(zin2.at[zz], z2_r.at[zz])
            total = total + zin2[zz].astype(F32)

        for k in range(16):
            fo[:, k, :] = total[:, k * 128 : (k + 1) * 128]
        fb[...] = fo[...].astype(BF)
        for d in range(8):
            jj = (j + d) % 8
            part = fb.at[pl.ds((jj % 2) * 8 + (jj // 2) * 2, 2)]
            copies.append(send(part, fin_in.at[j], f_s.at[d], f_r.at[j], at(0, jj // 2, y, z, jj % 2)))
        for d in range(1, 8):
            jj = (j + d) % 8
            part = fb.at[pl.ds((jj % 2) * 8 + (jj // 2) * 2, 2)]
            copies.append(
                send(part, fin_in.at[j], f_s.at[7 + d], f_r.at[j], at(1, jj // 2, y, z, jj % 2))
            )
        fin_in[j] = fb[pl.ds(c * 8 + f * 2, 2)]
        for d in range(1, 8):
            jj = (j + d) % 8
            arrived(fin_in.at[jj], f_r.at[jj])
        out[...] = fin_in[...]
        for cp in copies:
            cp.wait_send()


def moved(m1_src, res_src, gain, ow, gw, uw, dw):
    def v(*shape, dtype=BF):
        return pltpu.VMEM(shape, dtype)

    scratch = [
        v(512, 4096), v(4096, 256), v(4096, 256), v(256, 4096),
        v(8, 32, 128), v(256, 128), v(256, 128), v(4, 256, 128),
        v(4, 64, 128), v(256, 128, dtype=F32), v(256, 256, dtype=F32),
        v(16, 128, 256, dtype=F32), v(16, 128, 256), v(16, 128, 256), v(16, 128, 256),
        v(2, 128, 256), v(2, 128, 256), v(4, 128, 256), v(4, 128, 256),
        v(4, 128, 256), v(4, 128, 256),
        v(16, 2, 128, 256), v(256, 512, dtype=F32), v(256, 128, dtype=F32),
        v(4, 64, 640), v(4, 64, 640), v(256, 256),
        v(4, 64, 2048, dtype=F32), v(4, 64, 2048), v(4, 64, 2048), v(4, 64, 2048),
        v(32, 2048), v(32, 2048), v(64, 2048), v(64, 2048),
        v(4, 16, 2048), v(4, 16, 2048),
        v(16, 16, 128, dtype=F32), v(16, 16, 128), v(8, 2, 16, 128),
    ]
    counts = [
        4, 8, 8, 16, 16, 4, 4, 4, 4, 4, 4, 6, 6, 4, 4,
        4, 12, 16, 16, 16, 4, 4, 4, 4, 4, 4, 6, 6, 4, 4,
        15, 8,
    ]
    scratch += [pltpu.SemaphoreType.DMA((k,)) for k in counts]
    vm, hbm = pl.BlockSpec(memory_space=pltpu.VMEM), pl.BlockSpec(memory_space=pl.ANY)
    return pl.pallas_call(
        kernel,
        out_shape=jax.ShapeDtypeStruct((8, 2, 16, 128), BF),
        in_specs=[vm, vm, vm, hbm, hbm, hbm, hbm],
        out_specs=vm,
        scratch_shapes=scratch,
        compiler_params=pltpu.CompilerParams(
            collective_id=0, has_side_effects=True, vmem_limit_bytes=56 * 1024 * 1024
        ),
    )(m1_src, res_src, gain, ow, gw, uw, dw)


def on_device(
    queries, new_entries, cached_entries, lengths, residual, norm_gain,
    out_weight, gate_weight, up_weight, down_weight,
):
    mixed = attend(queries, new_entries, cached_entries[0], lengths)
    m1_src = mixed.reshape(2, 16, 2, 4, 128).transpose(3, 2, 0, 1, 4).reshape(8, 32, 128)
    res_src = residual.reshape(2, 4, 32, 128).transpose(1, 0, 2, 3).reshape(4, 64, 128)
    gain = norm_gain.astype(F32).reshape(16, 1, 256)
    res = moved(
        m1_src, res_src, gain, out_weight[0], gate_weight[0], up_weight[0], down_weight[0]
    )
    return res.transpose(1, 0, 2, 3).reshape(2, D)


def solution(mesh):
    placed = (
        P(("fin", "fhid"), None),
        P(("fin", "fhid"), None),
        P("side", ("fin", "fhid"), None, None),
        P(("fin", "fhid")),
        P(("fin", "fhid"), None),
        P("fin"),
        P("side", "fhid", "fin"),
        P("side", "fin", "fhid"),
        P("side", "fin", "fhid"),
        P("side", "fhid", "fin"),
    )
    return jax.shard_map(
        on_device, mesh=mesh, in_specs=placed, out_specs=P(("fin", "fhid"), None), check_vma=False
    )
```

time: 650 us -> 115 us (0.18)
  waiting for transfers between devices: 541 us -> 0 us
  Pallas kernels: 0 us -> 106 us
  blocking collectives: 51.1 us -> 0 us
  matrix products: 14.8 us -> 0.89 us
  between operations: 13.3 us -> 0.11 us
  starting transfers between devices: 12.6 us -> 0 us
  other arithmetic: 7.77 us -> 0.92 us
    psum x3 -> x0, waiting for transfers between devices: 376 us -> none  [the longest x1 293 us: layer(): projected = lax.psum(partial_value, 'fhid')]
    reduce_scatter x1 -> x0, waiting for transfers between devices: 151 us -> none  [layer(): lax.psum_scatter(jnp.dot(hidden, down_block, preferred_element_type=jnp.f...]
    pallas_call x0 -> x1, Pallas kernels: none -> 106 us  [moved(): pl.pallas_call(kernel, out_shape=jax.ShapeDtypeStruct((8, 2, 16, 128), BF...]
    all_to_all x2 -> x0, blocking collectives: 32.9 us -> none  [the longest x1 23.5 us: layer(): lax.all_to_all(grouped, 'fhid', split_axis=1, concat_axis=0, tiled=True)]
    dot_general x5 -> x1, matrix products: 14 us -> 0.14 us  [attend(): jnp.einsum('rgqd,rgd->rgq', heads, new_key, preferred_element_type=F32)]
    all_gather x1 -> x0, blocking collectives: 9.36 us -> none  [layer(): grouped = lax.all_gather(arrived, 'fin', axis=0, tiled=True)]
    ppermute x1 -> x0, starting transfers between devices: 8.82 us -> none  [passed_along(): return lax.ppermute(block, axis, route)]
    psum x1 -> x0, blocking collectives: 8.78 us -> none  [layer(): total_square = lax.psum(jnp.sum(stream_wide * stream_wide, axis=1), 'fin')]
  transfers between devices with their start and end apart: 7 -> 0, of which waited for: 7 -> 0; matrix products, arithmetic and copies ran while one was open for 2% -> 0% of each run, Pallas kernels for 0% -> 0%
where the time goes in v1:
time: 115 us
  Pallas kernels  106 us (92%)
  local copies, waits for them, and re-layouts  6.52 us (6%)
    pallas_call x1, Pallas kernels, moved(): pl.pallas_call(kernel, out_shape=jax.ShapeDtypeStruct((8, 2, 16, 128), BF...  106 us
    unnamed x15, local copies, waits for them, and re-layouts  4.24 us

profile of v1, /device:TPU:1, one launch (start us, length us, event | category | flops | bytes accessed | tf_op | source)
XLA Modules:
  0.0 114.8 jit_solution(9942753511756711311)
XLA Ops:
  0.0 2.8 %copy.13 = bf16[1,2,256,2048]{2,3,1,0:T(8,128)(2,1)S(1)} copy(bf16[1,2,256,2048]{3,2,1,0:T(8,128)(2,1)} %param.12) | data formatting | bytes 4194304 | tf_op args[2]
  2.9 0.0 copy-start
  2.9 0.0 copy-start.4
  2.9 0.0 copy-start.3
  2.9 0.1 fusion.7
  3.0 0.0 copy-start.1
  3.0 0.6 copy-done
  3.7 0.0 copy-start.2
  3.7 0.0 copy-done.4
  3.7 0.1 iota_compare_fusion
  3.8 0.3 fusion.8
  4.1 0.0 copy-done.3
  4.2 0.1 fusion.9
  4.3 0.2 fusion.2
  4.6 0.4 fusion.1
  5.0 0.7 copy.16
  5.6 0.0 copy-done.1
  5.7 0.6 copy.17
  6.3 0.0 copy-done.2
  6.3 0.6 reshape.72
  6.9 106.3 %shard_map.100 = bf16[8,2,16,128]{3,2,1,0:T(8,128)(2,1)} custom-call(bf16[8,32,128]{2,1,0:T(8,128)(2,1)} %bitcast.46, bf16[4,64,128]{2,1,0:T(8,128)(2,1)} %bitcast.47, f32[16,1,256]{2,1,0:T(1,128)} %bitcast.53, bf16[512,4096]{1,0:T(8,128)(2,1)} %bitcast.40, bf16[4096,256]{1,0:T(8,128)(2,1)} %bitcast.42, bf16[4096,256]{1,0:T(8,128)(2,1)} %bitcast.43, ...), custom_call_target="tpu_custom_call" | custom-call | tf_op jit(solution)/shard_map/pallas_call | solution.py:464
  113.2 0.8 copy.18
  114.1 0.7 copy.29
  (7 shorter events, 0.1 us)
Async XLA Ops:
  2.9 0.8 copy-start
  2.9 0.8 copy-start.4
  2.9 1.2 %copy-start.3 = (bf16[2,2048]{1,0:T(2,128)(2,1)S(1)}, bf16[2,2048]{1,0:T(2,128)(2,1)}, u32[]{:S(2)}) copy-start(bf16[2,2048]{1,0:T(2,128)(2,1)} %param.11) | copy-start | bytes 24580
  3.0 2.6 %copy-start.1 = (bf16[2,16384]{1,0:T(2,128)(2,1)S(1)}, bf16[2,16384]{1,0:T(2,128)(2,1)}, u32[]{:S(2)}) copy-start(bf16[2,16384]{1,0:T(2,128)(2,1)} %param.14) | copy-start | bytes 196612
  3.7 2.6 %copy-start.2 = (bf16[4096]{0:T(1024)(128)(2,1)S(1)}, bf16[4096]{0:T(1024)(128)(2,1)}, u32[]{:S(2)}) copy-start(bf16[4096]{0:T(1024)(128)(2,1)} %param.15) | copy-start | bytes 24580

commit v2 on v0

v2 whole, which is shorter than its diff:
```python
import math

import jax
import jax.numpy as jnp
from jax import lax
from jax.experimental import pallas as pl
from jax.experimental.pallas import tpu as pltpu
from jax.sharding import PartitionSpec as P

D = 16384
BF = jnp.bfloat16
F32 = jnp.float32
MESH = pl.DeviceIdType.MESH
ORDER = (2, 1, 3, 0)


def iota(shape, axis):
    return lax.broadcasted_iota(jnp.int32, shape, axis)


def selection(source, rows=256):
    t = iota((rows, 256), 0)
    return (iota((rows, 256), 1) == source(t)).astype(F32).astype(BF)


def arrived(ref, sem):
    pltpu.make_async_copy(ref, ref, sem).wait()


def attend(q, fresh, lens, kv, kv_copies, sco):
    scale = 1.0 / math.sqrt(128)
    for i in range(2):
        kv_copies[i * 2].wait()
        for g in range(8):
            at = (i * 8 + g) * 16
            sco[at : at + 16, :] = lax.dot_general(
                q[at : at + 16, :],
                kv[i, :, g * 128 : (g + 1) * 128],
                (((1,), (1,)), ((), ())),
                preferred_element_type=F32,
            )
    first = iota((256, 1), 0) < 128
    length = jnp.where(first, lens[0], lens[1])
    scores = jnp.where(iota((256, 256), 1) < length, sco[...] * scale, jnp.float32(-1e30))

    def spread(offset):
        rows = [
            jnp.broadcast_to(fresh[i * 16 + offset + g : i * 16 + offset + g + 1, :], (16, 128))
            for i in range(2)
            for g in range(8)
        ]
        return jnp.concatenate(rows, axis=0)

    own = jnp.sum(q[...].astype(F32) * spread(0), axis=1, keepdims=True) * scale
    top = jnp.maximum(jnp.max(scores, axis=1, keepdims=True), own)
    expo = jnp.exp(scores - top)
    own_exp = jnp.exp(own - top)
    total = jnp.sum(expo, axis=1, keepdims=True) + own_exp
    weights = (expo / total).astype(BF)
    own_weight = (own_exp / total).astype(BF).astype(F32)
    parts = []
    for i in range(2):
        kv_copies[i * 2 + 1].wait()
        for g in range(8):
            at = (i * 8 + g) * 16
            parts.append(
                jnp.dot(
                    weights[at : at + 16, :],
                    kv[i, :, 1024 + g * 128 : 1024 + (g + 1) * 128],
                    preferred_element_type=F32,
                )
            )
    return (jnp.concatenate(parts, axis=0) + own_weight * spread(8)).astype(BF)


def kernel(
    q_hbm, fresh_hbm, lens, kv_hbm, res_hbm, gain_hbm, ow_hbm, gw_hbm, uw_hbm, dw_hbm, out,
    wide, wide_f, narrow, narrow_f, q, res_src, gain_in, gain, fin_f,
    kv, sco, m1s, m1, comb, m2s,
    ow, gw, uw, dw, m2, m2all, lhs, rin, resid, acc,
    own, cs, cr, qs, ya, yb, yfm, yfp, zs, zin, tot,
    sbuf, gu, ss, xs, xr, hid,
    own2, cs2, cr2, qs2, ya2, yb2, yfm2, yfp2, zs2, zin2, tot2, fo, fb, fin_in,
    in_sem, w_sem, kv_sem, m1_s, m1_r, m2_s, m2_r, rs_s, rs_r, xa_s, xa_r,
    c_s, c_r, y_s, y_r, z_s, z_r, az_s, ay_s, ac_s, ag_r, ac_r,
    xs_s, xs_r, xh_s, xh_r, c2_s, c2_r, y2_s, y2_r, z2_s, z2_r, f_s, f_r,
):
    side, f, h = lax.axis_index("side"), lax.axis_index("fin"), lax.axis_index("fhid")
    y, z, c = h // 8, (h // 2) % 4, h % 2
    yz = h // 2
    oc = 1 - c
    j = f * 2 + c
    zt = 3 - z
    copies = []

    def at(s, ff, yy, zz, cc):
        return (s, ff, (yy * 4 + zz) * 2 + cc)

    def send(src, dst, s_sem, r_sem, dev):
        cp = pltpu.make_async_remote_copy(
            src_ref=src, dst_ref=dst, send_sem=s_sem, recv_sem=r_sem,
            device_id=dev, device_id_type=MESH,
        )
        cp.start()
        copies.append(cp)

    barrier = pltpu.get_barrier_semaphore()

    def greet(dev):
        pl.semaphore_signal(barrier, inc=1, device_id=dev, device_id_type=MESH)

    def deliver():
        for s in range(8):
            arrived(fin_in.at[s], f_r.at[s])
        fin_f[...] = fin_in[...].astype(F32)
        parts = [fin_f[s, :, k, :] for s in range(8) for k in range(16)]
        out[...] = jnp.concatenate(parts, axis=1).astype(BF)

    @pl.when(side == 0)
    def _attention_side():
        kv_copies = []
        for i in range(2):
            for k in range(2):
                part = (i, slice(None), pl.ds(k * 1024, 1024))
                cp = pltpu.make_async_copy(kv_hbm.at[part], kv.at[part], kv_sem.at[i * 2 + k])
                cp.start()
                kv_copies.append(cp)
        first_in = pltpu.make_async_copy(q_hbm, wide, in_sem.at[0])
        second_in = pltpu.make_async_copy(fresh_hbm, narrow, in_sem.at[1])
        first_in.start()
        second_in.start()
        greet(at(0, f, y, z, oc))
        for d in range(8):
            greet(at(1, d // 2, y, zt, d % 2))
        first_in.wait()
        second_in.wait()
        value = wide[...].astype(F32)
        for k in range(128):
            wide_f[:, k, :] = value[:, k * 128 : (k + 1) * 128]
        q[...] = wide_f[...].reshape(256, 128).astype(BF)
        value = narrow[...].astype(F32)
        for k in range(16):
            narrow_f[:, k, :] = value[:, k * 128 : (k + 1) * 128]
        fresh = narrow_f[...].reshape(32, 128)
        mixed = attend(q, fresh, lens, kv, kv_copies, sco)
        sel = selection(
            lambda t: (t // 4) % 2 * 128 + (t // 8) % 16 * 8 + (t // 128 + c) % 2 * 4 + t % 4
        )
        moved_rows = jnp.dot(sel, mixed, preferred_element_type=F32)
        m1s[...] = moved_rows[128:, :].astype(BF)
        comb[:, pl.ds(pl.multiple_of(c * 8, 8), 8), :] = moved_rows[:128, :].reshape(16, 8, 128)
        pl.semaphore_wait(barrier, 17)
        send(m1s, m1, m1_s, m1_r, at(0, f, y, z, oc))
        arrived(m1, m1_r)
        comb[:, pl.ds(pl.multiple_of(oc * 8, 8), 8), :] = m1[...].astype(F32).reshape(16, 8, 128)
        m2s[...] = comb[...].reshape(256, 128).astype(BF)
        for b in range(16):
            send(
                m2s.at[pl.ds(b * 16, 16)],
                m2.at[pl.ds(pl.multiple_of(yz * 16, 16), 16)],
                m2_s.at[b],
                m2_r.at[yz],
                at(1, f, b // 4, b % 4, c),
            )
        for cp in copies:
            cp.wait_send()
        deliver()

    @pl.when(side == 1)
    def _mlp_side():
        copies.clear()
        up, down, far = (y + 1) % 4, (y + 3) % 4, (y + 2) % 4
        dev_up, dev_down = at(1, f, up, z, c), at(1, f, down, z, c)
        dev_core = at(1, f, y, z, oc)
        first_in = pltpu.make_async_copy(res_hbm, wide, in_sem.at[0])
        second_in = pltpu.make_async_copy(gain_hbm, gain_in, in_sem.at[1])
        first_in.start()
        second_in.start()
        for d in range(16):
            greet(at(0, f, d // 4, d % 4, c))
        for d in range(1, 4):
            greet(at(1, (f + d) % 4, y, z, c))
            greet(at(1, f, y, (z + d) % 4, c))
        greet(dev_up)
        greet(dev_down)
        greet(dev_core)
        for d in range(8):
            greet(at(1, d // 2, y, zt, d % 2))
        weights = [
            pltpu.make_async_copy(a, b, w_sem.at[k])
            for k, (a, b) in enumerate(((ow_hbm, ow), (gw_hbm, gw), (uw_hbm, uw), (dw_hbm, dw)))
        ]
        for cp in weights:
            cp.start()
        gu[...] = jnp.zeros_like(gu)
        ss[...] = jnp.zeros_like(ss)
        first_in.wait()
        second_in.wait()
        value = wide[...].astype(F32)
        for k in range(128):
            wide_f[:, k, :] = value[:, k * 128 : (k + 1) * 128]
        for k in range(4):
            rows = wide_f[:, k * 32 : (k + 1) * 32, :]
            res_src[k] = rows.reshape(64, 128).astype(BF)
        gain[...] = gain_in[...].astype(F32).reshape(32, 128)
        pl.semaphore_wait(barrier, 25)

        for d in range(1, 4):
            ff = (f + d) % 4
            send(res_src.at[ff], rin.at[f], rs_s.at[d], rs_r.at[f], at(1, ff, y, z, c))
        rin[f] = res_src[f]
        for d in range(1, 4):
            ff = (f + d) % 4
            arrived(rin.at[ff], rs_r.at[ff])
        sel = selection(
            lambda t: (t // 2) % 4 * 64 + ((t % 2) * 16 + (t // 8) % 16) * 2 + t // 128
        )
        resid[...] = jnp.dot(sel, rin[...].reshape(256, 128), preferred_element_type=F32)

        pick = selection(
            lambda t: (t // 8) % 16 * 16 + (t // 128) % 2 * 8 + t % 2 * 4 + t // 256, 1024
        )
        row_fin = (iota((1024, 128), 0) // 2) % 4
        for s in range(16):
            arrived(m2.at[pl.ds(s * 16, 16)], m2_r.at[s])
        for d in range(1, 4):
            ff = (f + d) % 4
            send(m2, m2all.at[f], xa_s.at[d], xa_r.at[f], at(1, ff, y, z, c))
        picked = jnp.where(
            row_fin == f, jnp.dot(pick, m2[...], preferred_element_type=F32), 0.0
        )
        for d in (1, 3, 2):
            ff = (f + d) % 4
            arrived(m2all.at[ff], xa_r.at[ff])
            picked = jnp.where(
                row_fin == ff, jnp.dot(pick, m2all[ff], preferred_element_type=F32), picked
            )
        for k in range(4):
            lhs[:, k * 128 : (k + 1) * 128] = picked[k * 256 : (k + 1) * 256, :].astype(BF)
        weights[0].wait()

        def project(p, g):
            mine = (c == p).astype(F32)
            yy = (y + ORDER[g]) % 4

            def chunk(k, carry):
                n = yy * 4 + k
                w = ow[:, pl.ds(pl.multiple_of(n * 256, 256), 256)]
                acc[...] = jnp.dot(
                    lhs[p * 128 : (p + 1) * 128, :], w, preferred_element_type=F32
                )
                r8 = pl.ds(pl.multiple_of(yz * 8, 8), 8)
                lo = resid[pl.ds(pl.multiple_of(n * 8, 8), 8), :]
                hi = resid[pl.ds(pl.multiple_of(128 + n * 8, 8), 8), :]
                acc[r8, :] = acc[r8, :] + jnp.concatenate([lo, hi], axis=1) * mine
                own[p, n] = acc[pl.ds(pl.multiple_of(c * 64, 64), 64), :]
                cs[p, n] = acc[pl.ds(pl.multiple_of(oc * 64, 64), 64), :].astype(BF)
                return carry

            lax.fori_loop(0, 4, chunk, 0)
            part = pl.ds(yy * 4, 4)
            send(cs.at[p, part], cr.at[p, part], c_s.at[p, g], c_r.at[p, g], dev_core)

        a, b = pl.ds(0, 2), pl.ds(2, 2)

        def paired(p, yy, half):
            part = pl.ds(yy * 4 + half * 2, 2)
            return own[p, part] + cr[p, part].astype(F32)

        def opposite(p):
            arrived(cr.at[p, pl.ds(far * 4, 4)], c_r.at[p, 0])
            qs[p, far, a] = paired(p, far, 0).astype(BF)
            send(qs.at[p, far, a], ya.at[p], y_s.at[p, 0], y_r.at[p, 0], dev_up)
            qs[p, far, b] = paired(p, far, 1).astype(BF)
            send(qs.at[p, far, b], yb.at[p], y_s.at[p, 1], y_r.at[p, 1], dev_down)

        def beside(p):
            arrived(cr.at[p, pl.ds(up * 4, 4)], c_r.at[p, 1])
            qs[p, up, b] = paired(p, up, 1).astype(BF)
            send(qs.at[p, up, b], yfm.at[p, b], y_s.at[p, 2], y_r.at[p, 2], dev_up)
            arrived(cr.at[p, pl.ds(down * 4, 4)], c_r.at[p, 2])
            qs[p, down, a] = paired(p, down, 0).astype(BF)
            send(qs.at[p, down, a], yfp.at[p, a], y_s.at[p, 3], y_r.at[p, 3], dev_down)

        def onward(p):
            arrived(ya.at[p], y_r.at[p, 0])
            qs[p, up, a] = (paired(p, up, 0) + ya[p].astype(F32)).astype(BF)
            send(qs.at[p, up, a], yfm.at[p, a], y_s.at[p, 4], y_r.at[p, 4], dev_up)
            arrived(yb.at[p], y_r.at[p, 1])
            qs[p, down, b] = (paired(p, down, 1) + yb[p].astype(F32)).astype(BF)
            send(qs.at[p, down, b], yfp.at[p, b], y_s.at[p, 5], y_r.at[p, 5], dev_down)

        def over_z(p):
            part = pl.ds(y * 4, 4)
            arrived(cr.at[p, part], c_r.at[p, 3])
            arrived(yfm.at[p, b], y_r.at[p, 2])
            arrived(yfp.at[p, a], y_r.at[p, 3])
            arrived(yfm.at[p, a], y_r.at[p, 4])
            arrived(yfp.at[p, b], y_r.at[p, 5])

            def summed(k):
                value = own[p, y * 4 + k] + cr[p, y * 4 + k].astype(F32)
                return value + yfm[p, k].astype(F32) + yfp[p, k].astype(F32)

            for d in (2, 1, 3):
                zz = (z + d) % 4
                zs[p, zz] = summed(zz).astype(BF)
                send(zs.at[p, zz], zin.at[p, z], z_s.at[p, d], z_r.at[p, z], at(1, f, y, zz, c))
            tot[p] = summed(z)

        def give(p, n, slot, dev):
            ref = sbuf.at[p, n, c]
            send(ref, ref, ay_s.at[p, slot], ag_r.at[p, n], dev)

        def give_y(p, n, k):
            give(p, n, 2 * k, dev_up)
            give(p, n, 2 * k + 1, dev_down)

        def give_core(p, n):
            ref = sbuf.at[p, n, c]
            send(ref, ref, ac_s.at[p, n], ac_r.at[p, n], dev_core)

        def use(p, n):
            arrived(sbuf.at[p, n, oc], ac_r.at[p, n])
            x = sbuf[p, n].reshape(128, 256).astype(F32)
            sq = x * x
            ss[p] += sq[:, :128] + sq[:, 128:]
            pair = [gain[pl.ds(n * 2 + k, 1), :] for k in range(2)]
            xg = (x * jnp.concatenate(pair, axis=1)).astype(BF)
            rows = pl.ds(pl.multiple_of(n * 256, 256), 256)
            gu[p, :, :256] += jnp.dot(xg, gw[rows, :], preferred_element_type=F32)
            gu[p, :, 256:] += jnp.dot(xg, uw[rows, :], preferred_element_type=F32)

        def near(p):
            total = tot[p]
            for d in (1, 3, 2):
                zz = (z + d) % 4
                arrived(zin.at[p, zz], z_r.at[p, zz])
                total = total + zin[p, zz].astype(F32)
            sbuf[p, yz, c] = total.astype(BF)
            for d in (2, 1, 3):
                zz = (z + d) % 4
                ref = sbuf.at[p, yz, c]
                send(ref, ref, az_s.at[p, d], ag_r.at[p, yz], at(1, f, y, zz, c))
            give_y(p, yz, 0)
            give_core(p, yz)

        def forward(p):
            for d in range(1, 4):
                n = y * 4 + (z + d) % 4
                arrived(sbuf.at[p, n, c], ag_r.at[p, n])
                give_y(p, n, d)
                give_core(p, n)

        def beside_arrived(p, d):
            n = down * 4 + (z + d) % 4
            arrived(sbuf.at[p, n, c], ag_r.at[p, n])
            if d % 2 == 0:
                give(p, n, 8 + d, dev_up)
            give_core(p, n)
            n = up * 4 + (z + d) % 4
            arrived(sbuf.at[p, n, c], ag_r.at[p, n])
            if d % 2 == 1:
                give(p, n, 8 + d, dev_down)
            give_core(p, n)

        def opposite_arrived(p, d):
            n = far * 4 + (z + d) % 4
            arrived(sbuf.at[p, n, c], ag_r.at[p, n])
            give_core(p, n)

        def use_all(p, group):
            for d in range(4):
                use(p, group * 4 + (z + d) % 4)

        def over_fin(p):
            tt = jnp.sum(ss[p], axis=1, keepdims=True)
            top = tt.astype(BF).astype(F32)
            low = iota((128, 128), 1) < 64
            xs[p, :, :, 512:] = jnp.where(low, top, tt - top).astype(BF).reshape(4, 32, 128)
            xs[p, :, :, :512] = gu[p].astype(BF).reshape(4, 32, 512)
            for d in (2, 1, 3):
                ff = (f + d) % 4
                send(xs.at[p, ff], xr.at[p, f], xs_s.at[p, d], xs_r.at[p, f], at(1, ff, y, z, c))

        def hide(p):
            mine = pl.ds(pl.multiple_of(f * 32, 32), 32)
            both = gu[p, mine, :]
            square = xs[p, f][:, 512:].astype(F32)
            for d in (1, 3, 2):
                ff = (f + d) % 4
                arrived(xr.at[p, ff], xs_r.at[p, ff])
                both = both + xr[p, ff][:, :512].astype(F32)
                square = square + xr[p, ff][:, 512:].astype(F32)
            scale = lax.rsqrt((square[:, 0:1] + square[:, 64:65]) / D + 1e-05)
            gate = both[:, :256] * scale
            hid[p, mine, :] = (gate / (1.0 + jnp.exp(-gate)) * (both[:, 256:] * scale)).astype(BF)
            for d in (2, 1, 3):
                ff = (f + d) % 4
                ref = hid.at[p, mine]
                send(ref, ref, xh_s.at[p, d], xh_r.at[p, f], at(1, ff, y, z, c))

        def lower(p):
            for d in (1, 3, 2):
                ff = (f + d) % 4
                ref = hid.at[p, pl.ds(pl.multiple_of(ff * 32, 32), 32)]
                arrived(ref, xh_r.at[p, ff])

            def columns(core, k):
                parts = []
                for half in range(2):
                    start = core * 2048 + half * 1024 + k * 512
                    w = dw[:, pl.ds(pl.multiple_of(start, 512), 512)]
                    value = jnp.dot(hid[p], w, preferred_element_type=F32)
                    parts.append(value.reshape(16, 8, 512))
                return jnp.concatenate(parts, axis=1)

            for k in range(2):
                cs2[p, :, :, k * 512 : (k + 1) * 512] = columns(oc, k).astype(BF)
            for g in range(4):
                part = pl.ds((y + ORDER[g]) % 4 * 4, 4)
                send(cs2.at[p, part], cr2.at[p, part], c2_s.at[p, g], c2_r.at[p, g], dev_core)
            for k in range(2):
                own2[p, :, :, k * 512 : (k + 1) * 512] = columns(c, k)

        def paired2(p, yy, half):
            part = pl.ds(yy * 4 + half * 2, 2)
            return own2[p, part] + cr2[p, part].astype(F32)

        def opposite2(p):
            arrived(cr2.at[p, pl.ds(far * 4, 4)], c2_r.at[p, 0])
            qs2[p, far, a] = paired2(p, far, 0).astype(BF)
            send(qs2.at[p, far, a], ya2.at[p], y2_s.at[p, 0], y2_r.at[p, 0], dev_up)
            qs2[p, far, b] = paired2(p, far, 1).astype(BF)
            send(qs2.at[p, far, b], yb2.at[p], y2_s.at[p, 1], y2_r.at[p, 1], dev_down)

        def beside2(p):
            arrived(cr2.at[p, pl.ds(up * 4, 4)], c2_r.at[p, 1])
            qs2[p, up, b] = paired2(p, up, 1).astype(BF)
            send(qs2.at[p, up, b], yfm2.at[p, b], y2_s.at[p, 2], y2_r.at[p, 2], dev_up)
            arrived(cr2.at[p, pl.ds(down * 4, 4)], c2_r.at[p, 2])
            qs2[p, down, a] = paired2(p, down, 0).astype(BF)
            send(qs2.at[p, down, a], yfp2.at[p, a], y2_s.at[p, 3], y2_r.at[p, 3], dev_down)

        def onward2(p):
            arrived(ya2.at[p], y2_r.at[p, 0])
            qs2[p, up, a] = (paired2(p, up, 0) + ya2[p].astype(F32)).astype(BF)
            send(qs2.at[p, up, a], yfm2.at[p, a], y2_s.at[p, 4], y2_r.at[p, 4], dev_up)
            arrived(yb2.at[p], y2_r.at[p, 1])
            qs2[p, down, b] = (paired2(p, down, 1) + yb2[p].astype(F32)).astype(BF)
            send(qs2.at[p, down, b], yfp2.at[p, b], y2_s.at[p, 5], y2_r.at[p, 5], dev_down)

        def over_z2(p):
            part = pl.ds(y * 4, 4)
            arrived(cr2.at[p, part], c2_r.at[p, 3])
            arrived(yfm2.at[p, b], y2_r.at[p, 2])
            arrived(yfp2.at[p, a], y2_r.at[p, 3])
            arrived(yfm2.at[p, a], y2_r.at[p, 4])
            arrived(yfp2.at[p, b], y2_r.at[p, 5])

            def summed(k):
                value = own2[p, y * 4 + k] + cr2[p, y * 4 + k].astype(F32)
                return value + yfm2[p, k].astype(F32) + yfp2[p, k].astype(F32)

            for d in (2, 1, 3):
                zz = (z + d) % 4
                zs2[p, zz] = summed(3 - zz).astype(BF)
                send(
                    zs2.at[p, zz], zin2.at[p, z], z2_s.at[p, d], z2_r.at[p, z], at(1, f, y, zz, c)
                )
            slab = pl.ds(pl.multiple_of(((y * 4 + zt) % 8) // 2 * 16, 16), 16)
            halves = []
            for half in range(2):
                kept = [
                    sbuf[p, c * 8 + half * 4 + m, y // 2, slab, :].astype(F32) for m in range(4)
                ]
                kept = jnp.concatenate(kept, axis=1)
                halves.append(jnp.where(zt % 2 == 0, kept[:8], kept[8:]))
            tot2[p] = summed(zt) + jnp.concatenate(halves, axis=0)

        def finish(p):
            total = tot2[p]
            for d in (1, 3, 2):
                zz = (z + d) % 4
                arrived(zin2.at[p, zz], z2_r.at[p, zz])
                total = total + zin2[p, zz].astype(F32)
            for k in range(16):
                rows = slice(k // 8 * 8, k // 8 * 8 + 8)
                fo[:, k, :] = total[rows, k % 8 * 128 : (k % 8 + 1) * 128]
            fb[p] = fo[...].astype(BF)
            for d in range(8):
                ff = (f + d // 2) % 4
                send(
                    fb.at[p, pl.ds(ff * 2, 2)], fin_in.at[j], f_s.at[p, d], f_r.at[j],
                    at(d % 2, ff, y, zt, p),
                )

        project(0, 0)
        project(1, 0)
        opposite(0)
        project(0, 1)
        opposite(1)
        project(0, 2)
        project(1, 1)
        beside(0)
        project(1, 2)
        project(0, 3)
        beside(1)
        project(1, 3)
        onward(0)
        onward(1)
        over_z(0)
        over_z(1)
        near(0)
        near(1)
        weights[1].wait()
        weights[2].wait()
        forward(0)
        forward(1)
        for d in range(4):
            beside_arrived(0, d)
            use(0, y * 4 + (z + d) % 4)
        for d in range(4):
            beside_arrived(1, d)
            use(0, down * 4 + (z + d) % 4)
            use(0, up * 4 + (z + d) % 4)
        for d in range(4):
            opposite_arrived(0, d)
            use(1, y * 4 + (z + d) % 4)
        use_all(0, far)
        over_fin(0)
        for d in range(4):
            opposite_arrived(1, d)
            use(1, down * 4 + (z + d) % 4)
            use(1, up * 4 + (z + d) % 4)
        use_all(1, far)
        over_fin(1)
        hide(0)
        hide(1)
        weights[3].wait()
        lower(0)
        opposite2(0)
        beside2(0)
        lower(1)
        opposite2(1)
        beside2(1)
        onward2(0)
        onward2(1)
        over_z2(0)
        over_z2(1)
        finish(0)
        finish(1)
        deliver()
        for cp in copies:
            cp.wait_send()


def moved(*args):
    def v(*shape, dtype=BF):
        return pltpu.VMEM(shape, dtype)

    scratch = [
        v(2, D), v(2, 128, 128, dtype=F32), v(2, 2048), v(2, 16, 128, dtype=F32), v(256, 128),
        v(4, 64, 128), v(4096), v(32, 128, dtype=F32), v(8, 2, 16, 128, dtype=F32),
        v(2, 256, 2048), v(256, 256, dtype=F32), v(128, 128), v(128, 128),
        v(16, 16, 128, dtype=F32), v(256, 128),
        v(512, 4096), v(4096, 256), v(4096, 256), v(256, 4096),
        v(256, 128), v(4, 256, 128), v(256, 512),
        v(4, 64, 128), v(256, 128, dtype=F32), v(128, 256, dtype=F32),
        v(2, 16, 64, 256, dtype=F32), v(2, 16, 64, 256), v(2, 16, 64, 256), v(2, 4, 4, 64, 256),
        v(2, 2, 64, 256), v(2, 2, 64, 256), v(2, 4, 64, 256), v(2, 4, 64, 256),
        v(2, 4, 64, 256), v(2, 4, 64, 256), v(2, 64, 256, dtype=F32),
        v(2, 16, 2, 64, 256), v(2, 128, 512, dtype=F32), v(2, 128, 128, dtype=F32),
        v(2, 4, 32, 640), v(2, 4, 32, 640), v(2, 128, 256),
        v(2, 16, 16, 1024, dtype=F32), v(2, 16, 16, 1024), v(2, 16, 16, 1024),
        v(2, 4, 4, 16, 1024), v(2, 2, 16, 1024), v(2, 2, 16, 1024),
        v(2, 4, 16, 1024), v(2, 4, 16, 1024), v(2, 4, 16, 1024), v(2, 4, 16, 1024),
        v(2, 16, 1024, dtype=F32), v(8, 16, 128, dtype=F32), v(2, 8, 16, 128), v(8, 2, 16, 128),
    ]
    counts = [
        (2,), (4,), (4,), (), (), (16,), (16,), (4,), (4,), (4,), (4,),
        (2, 4), (2, 4), (2, 6), (2, 6), (2, 4), (2, 4),
        (2, 4), (2, 12), (2, 16), (2, 16), (2, 16),
        (2, 4), (2, 4), (2, 4), (2, 4), (2, 4), (2, 4), (2, 6), (2, 6), (2, 4), (2, 4),
        (2, 8), (8,),
    ]
    scratch += [pltpu.SemaphoreType.DMA(k) for k in counts]
    vm, hbm = pl.BlockSpec(memory_space=pltpu.VMEM), pl.BlockSpec(memory_space=pl.ANY)
    sm = pl.BlockSpec(memory_space=pltpu.SMEM)
    return pl.pallas_call(
        kernel,
        out_shape=jax.ShapeDtypeStruct((2, D), BF),
        in_specs=[hbm, hbm, sm, hbm, hbm, hbm, hbm, hbm, hbm, hbm],
        out_specs=vm,
        scratch_shapes=scratch,
        compiler_params=pltpu.CompilerParams(
            collective_id=0, has_side_effects=True, vmem_limit_bytes=56 * 1024 * 1024
        ),
    )(*args)


def on_device(
    queries, new_entries, cached_entries, lengths, residual, norm_gain,
    out_weight, gate_weight, up_weight, down_weight,
):
    return moved(
        queries, new_entries, lengths, cached_entries[0], residual, norm_gain,
        out_weight[0], gate_weight[0], up_weight[0], down_weight[0],
    )


def solution(mesh):
    placed = (
        P(("fin", "fhid"), None),
        P(("fin", "fhid"), None),
        P("side", ("fin", "fhid"), None, None),
        P(("fin", "fhid")),
        P(("fin", "fhid"), None),
        P("fin"),
        P("side", "fhid", "fin"),
        P("side", "fin", "fhid"),
        P("side", "fin", "fhid"),
        P("side", "fhid", "fin"),
    )
    return jax.shard_map(
        on_device, mesh=mesh, in_specs=placed, out_specs=P(("fin", "fhid"), None), check_vma=False
    )
```

time: 650 us -> 96 us (0.15)
  waiting for transfers between devices: 541 us -> 0 us
  Pallas kernels: 0 us -> 94.3 us
  blocking collectives: 51.1 us -> 0 us
  matrix products: 14.8 us -> 0 us
  between operations: 13.3 us -> 0.01 us
  starting transfers between devices: 12.6 us -> 0 us
  local copies, waits for them, and re-layouts: 9.57 us -> 1.52 us
  other arithmetic: 7.77 us -> 0 us
    psum x3 -> x0, waiting for transfers between devices: 376 us -> none  [the longest x1 293 us: layer(): projected = lax.psum(partial_value, 'fhid')]
    reduce_scatter x1 -> x0, waiting for transfers between devices: 151 us -> none  [layer(): lax.psum_scatter(jnp.dot(hidden, down_block, preferred_element_type=jnp.f...]
    pallas_call x0 -> x1, Pallas kernels: none -> 94.3 us  [moved(): pl.pallas_call(kernel, out_shape=jax.ShapeDtypeStruct((2, D), BF), in_spe...]
    all_to_all x2 -> x0, blocking collectives: 32.9 us -> none  [the longest x1 23.5 us: layer(): lax.all_to_all(grouped, 'fhid', split_axis=1, concat_axis=0, tiled=True)]
    dot_general x7 -> x0, matrix products: 14.8 us -> none  [the longest x1 5.46 us: layer(): jnp.dot(head_rows, out_block, preferred_element_type=jnp.float32)]
    all_gather x1 -> x0, blocking collectives: 9.36 us -> none  [layer(): grouped = lax.all_gather(arrived, 'fin', axis=0, tiled=True)]
    ppermute x1 -> x0, starting transfers between devices: 8.82 us -> none  [passed_along(): return lax.ppermute(block, axis, route)]
    psum x1 -> x0, blocking collectives: 8.78 us -> none  [layer(): total_square = lax.psum(jnp.sum(stream_wide * stream_wide, axis=1), 'fin')]
  transfers between devices with their start and end apart: 7 -> 0, of which waited for: 7 -> 0; matrix products, arithmetic and copies ran while one was open for 2% -> 0% of each run, Pallas kernels for 0% -> 0%
where the time goes in v2:
time: 96 us; the launch traced here: 95.9 us
  Pallas kernels  94.3 us (98%)
  local copies, waits for them, and re-layouts  1.52 us (2%)
    pallas_call x1, Pallas kernels, moved(): pl.pallas_call(kernel, out_shape=jax.ShapeDtypeStruct((2, D), BF), in_spe...  94.3 us

profile of v2, /device:TPU:1, one launch (start us, length us, event | category | flops | bytes accessed | tf_op | source)
XLA Modules:
  0.0 95.9 jit_solution(236251216728604088)
XLA Ops:
  0.0 94.3 %shard_map.100 = bf16[2,16384]{1,0:T(2,128)(2,1)} custom-call(bf16[2,16384]{1,0:T(2,128)(2,1)} %q_hbm.1, bf16[2,2048]{1,0:T(2,128)(2,1)} %fresh_hbm.1, s32[2]{0:T(128)} %lens.1, bf16[2,256,2048]{2,1,0:T(8,128)(2,1)} %bitcast.6, bf16[2,16384]{1,0:T(2,128)(2,1)} %res_hbm.1, bf16[4096]{0:T(1024)(128)(2,1)} %gain_hbm.1, bf16[512,4096]{1,0:T(8,128)(2,1)} %bitcast.5, ...), custom_call_target="tpu_custom_call" | custom-call | tf_op jit(solution)/shard_map/pallas_call | solution.py:590
  94.4 1.5 %copy.12 = bf16[2,16384]{1,0:T(2,128)(2,1)} copy(bf16[2,16384]{1,0:T(2,128)(2,1)} %shard_map.100) | data formatting | bytes 131072

commit v3 on v2

--- a/solution.py
+++ b/solution.py
@@ -11,7 +11,7 @@
 BF = jnp.bfloat16
 F32 = jnp.float32
 MESH = pl.DeviceIdType.MESH
-ORDER = (2, 1, 3, 0)
+ORDER = (1, 3, 2, 0)
 
 
 def iota(shape, axis):
@@ -78,12 +78,12 @@
     wide, wide_f, narrow, narrow_f, q, res_src, gain_in, gain, fin_f,
     kv, sco, m1s, m1, comb, m2s,
     ow, gw, uw, dw, m2, m2all, lhs, rin, resid, acc,
-    own, cs, cr, qs, ya, yb, yfm, yfp, zs, zin, tot,
+    own, cs, cr, qs, zfar, fs, ffar, yfm, yfp, zs, zin, tot,
     sbuf, gu, ss, xs, xr, hid,
-    own2, cs2, cr2, qs2, ya2, yb2, yfm2, yfp2, zs2, zin2, tot2, fo, fb, fin_in,
+    own2, cs2, cr2, qs2, zfar2, fs2, ffar2, yfm2, yfp2, zs2, zin2, tot2, fo, fb, fin_in,
     in_sem, w_sem, kv_sem, m1_s, m1_r, m2_s, m2_r, rs_s, rs_r, xa_s, xa_r,
-    c_s, c_r, y_s, y_r, z_s, z_r, az_s, ay_s, ac_s, ag_r, ac_r,
-    xs_s, xs_r, xh_s, xh_r, c2_s, c2_r, y2_s, y2_r, z2_s, z2_r, f_s, f_r,
+    c_s, c_r, y_s, y_r, z_s, z_r, zf_s, zf_r, az_s, ay_s, ac_s, ag_r, ac_r,
+    xs_s, xs_r, xh_s, xh_r, c2_s, c2_r, y2_s, y2_r, z2_s, z2_r, zf2_s, zf2_r, f_s, f_r,
 ):
     side, f, h = lax.axis_index("side"), lax.axis_index("fin"), lax.axis_index("fhid")
     y, z, c = h // 8, (h // 2) % 4, h % 2
@@ -170,7 +170,7 @@
     def _mlp_side():
         copies.clear()
         up, down, far = (y + 1) % 4, (y + 3) % 4, (y + 2) % 4
-        dev_up, dev_down = at(1, f, up, z, c), at(1, f, down, z, c)
+        dev_up, dev_down, dev_far = (at(1, f, yy, z, c) for yy in (up, down, far))
         dev_core = at(1, f, y, z, oc)
         first_in = pltpu.make_async_copy(res_hbm, wide, in_sem.at[0])
         second_in = pltpu.make_async_copy(gain_hbm, gain_in, in_sem.at[1])
@@ -183,6 +183,7 @@
             greet(at(1, f, y, (z + d) % 4, c))
         greet(dev_up)
         greet(dev_down)
+        greet(dev_far)
         greet(dev_core)
         for d in range(8):
             greet(at(1, d // 2, y, zt, d % 2))
@@ -203,7 +204,7 @@
             rows = wide_f[:, k * 32 : (k + 1) * 32, :]
             res_src[k] = rows.reshape(64, 128).astype(BF)
         gain[...] = gain_in[...].astype(F32).reshape(32, 128)
-        pl.semaphore_wait(barrier, 25)
+        pl.semaphore_wait(barrier, 26)
 
         for d in range(1, 4):
             ff = (f + d) % 4
@@ -221,17 +222,25 @@
             lambda t: (t // 8) % 16 * 16 + (t // 128) % 2 * 8 + t % 2 * 4 + t // 256, 1024
         )
         row_fin = (iota((1024, 128), 0) // 2) % 4
-        for s in range(16):
-            arrived(m2.at[pl.ds(s * 16, 16)], m2_r.at[s])
-        for d in range(1, 4):
-            ff = (f + d) % 4
-            send(m2, m2all.at[f], xa_s.at[d], xa_r.at[f], at(1, ff, y, z, c))
+        for e in (0, 1, 3, 2):
+            yy = (y + e) % 4
+            for k in range(4):
+                n = yy * 4 + k
+                arrived(m2.at[pl.ds(pl.multiple_of(n * 16, 16), 16)], m2_r.at[n])
+            part = pl.ds(pl.multiple_of(yy * 64, 64), 64)
+            for d in (2, 1, 3):
+                ff = (f + d) % 4
+                send(
+                    m2.at[part], m2all.at[f, part], xa_s.at[d, e], xa_r.at[f, yy],
+                    at(1, ff, y, z, c),
+                )
         picked = jnp.where(
             row_fin == f, jnp.dot(pick, m2[...], preferred_element_type=F32), 0.0
         )
         for d in (1, 3, 2):
             ff = (f + d) % 4
-            arrived(m2all.at[ff], xa_r.at[ff])
+            for k in range(4):
+                arrived(m2all.at[ff, pl.ds(k * 64, 64)], xa_r.at[ff, k])
             picked = jnp.where(
                 row_fin == ff, jnp.dot(pick, m2all[ff], preferred_element_type=F32), picked
             )
@@ -261,46 +270,44 @@
             part = pl.ds(yy * 4, 4)
             send(cs.at[p, part], cr.at[p, part], c_s.at[p, g], c_r.at[p, g], dev_core)
 
-        a, b = pl.ds(0, 2), pl.ds(2, 2)
-
-        def paired(p, yy, half):
-            part = pl.ds(yy * 4 + half * 2, 2)
-            return own[p, part] + cr[p, part].astype(F32)
+        def paired(p, n):
+            return own[p, n] + cr[p, n].astype(F32)
+
+        def beside(p, g):
+            yy = (y + ORDER[g]) % 4
+            part = pl.ds(yy * 4, 4)
+            arrived(cr.at[p, part], c_r.at[p, g])
+            qs[p, yy] = (own[p, part] + cr[p, part].astype(F32)).astype(BF)
+            to, dev = ((yfm, dev_up), (yfp, dev_down))[g]
+            send(qs.at[p, yy], to.at[p], y_s.at[p, g], y_r.at[p, g], dev)
 
         def opposite(p):
-            arrived(cr.at[p, pl.ds(far * 4, 4)], c_r.at[p, 0])
-            qs[p, far, a] = paired(p, far, 0).astype(BF)
-            send(qs.at[p, far, a], ya.at[p], y_s.at[p, 0], y_r.at[p, 0], dev_up)
-            qs[p, far, b] = paired(p, far, 1).astype(BF)
-            send(qs.at[p, far, b], yb.at[p], y_s.at[p, 1], y_r.at[p, 1], dev_down)
-
-        def beside(p):
-            arrived(cr.at[p, pl.ds(up * 4, 4)], c_r.at[p, 1])
-            qs[p, up, b] = paired(p, up, 1).astype(BF)
-            send(qs.at[p, up, b], yfm.at[p, b], y_s.at[p, 2], y_r.at[p, 2], dev_up)
-            arrived(cr.at[p, pl.ds(down * 4, 4)], c_r.at[p, 2])
-            qs[p, down, a] = paired(p, down, 0).astype(BF)
-            send(qs.at[p, down, a], yfp.at[p, a], y_s.at[p, 3], y_r.at[p, 3], dev_down)
+            arrived(cr.at[p, pl.ds(far * 4, 4)], c_r.at[p, 2])
+            for d in (2, 1, 3):
+                zz = (z + d) % 4
+                qs[p, far, zz] = paired(p, far * 4 + zz).astype(BF)
+                send(
+                    qs.at[p, far, zz], zfar.at[p, z], zf_s.at[p, d], zf_r.at[p, z],
+                    at(1, f, y, zz, c),
+                )
 
         def onward(p):
-            arrived(ya.at[p], y_r.at[p, 0])
-            qs[p, up, a] = (paired(p, up, 0) + ya[p].astype(F32)).astype(BF)
-            send(qs.at[p, up, a], yfm.at[p, a], y_s.at[p, 4], y_r.at[p, 4], dev_up)
-            arrived(yb.at[p], y_r.at[p, 1])
-            qs[p, down, b] = (paired(p, down, 1) + yb[p].astype(F32)).astype(BF)
-            send(qs.at[p, down, b], yfp.at[p, b], y_s.at[p, 5], y_r.at[p, 5], dev_down)
+            value = paired(p, far * 4 + z)
+            for d in (1, 3, 2):
+                zz = (z + d) % 4
+                arrived(zfar.at[p, zz], zf_r.at[p, zz])
+                value = value + zfar[p, zz].astype(F32)
+            fs[p] = value.astype(BF)
+            send(fs.at[p], ffar.at[p], y_s.at[p, 2], y_r.at[p, 2], dev_far)
 
         def over_z(p):
             part = pl.ds(y * 4, 4)
             arrived(cr.at[p, part], c_r.at[p, 3])
-            arrived(yfm.at[p, b], y_r.at[p, 2])
-            arrived(yfp.at[p, a], y_r.at[p, 3])
-            arrived(yfm.at[p, a], y_r.at[p, 4])
-            arrived(yfp.at[p, b], y_r.at[p, 5])
+            arrived(yfm.at[p], y_r.at[p, 0])
+            arrived(yfp.at[p], y_r.at[p, 1])
 
             def summed(k):
-                value = own[p, y * 4 + k] + cr[p, y * 4 + k].astype(F32)
-                return value + yfm[p, k].astype(F32) + yfp[p, k].astype(F32)
+                return paired(p, y * 4 + k) + yfm[p, k].astype(F32) + yfp[p, k].astype(F32)
 
             for d in (2, 1, 3):
                 zz = (z + d) % 4
@@ -337,12 +344,15 @@
                 zz = (z + d) % 4
                 arrived(zin.at[p, zz], z_r.at[p, zz])
                 total = total + zin[p, zz].astype(F32)
+            arrived(ffar.at[p], y_r.at[p, 2])
+            total = total + ffar[p].astype(F32)
             sbuf[p, yz, c] = total.astype(BF)
             for d in (2, 1, 3):
                 zz = (z + d) % 4
                 ref = sbuf.at[p, yz, c]
                 send(ref, ref, az_s.at[p, d], ag_r.at[p, yz], at(1, f, y, zz, c))
             give_y(p, yz, 0)
+            give(p, yz, 8, dev_far)
             give_core(p, yz)
 
         def forward(p):
@@ -352,25 +362,23 @@
                 give_y(p, n, d)
                 give_core(p, n)
 
-        def beside_arrived(p, d):
-            n = down * 4 + (z + d) % 4
+        def spread_opposite(p):
+            n = far * 4 + z
             arrived(sbuf.at[p, n, c], ag_r.at[p, n])
-            if d % 2 == 0:
-                give(p, n, 8 + d, dev_up)
+            for d in (2, 1, 3):
+                ref = sbuf.at[p, n, c]
+                send(
+                    ref, ref, az_s.at[p, 4 + d], ag_r.at[p, n], at(1, f, y, (z + d) % 4, c)
+                )
             give_core(p, n)
-            n = up * 4 + (z + d) % 4
-            arrived(sbuf.at[p, n, c], ag_r.at[p, n])
-            if d % 2 == 1:
-                give(p, n, 8 + d, dev_down)
-            give_core(p, n)
-
-        def opposite_arrived(p, d):
-            n = far * 4 + (z + d) % 4
+
+        def taken(p, group, d):
+            n = group * 4 + (z + d) % 4
             arrived(sbuf.at[p, n, c], ag_r.at[p, n])
             give_core(p, n)
 
-        def use_all(p, group):
-            for d in range(4):
+        def use_at(p, *places):
+            for group, d in places:
                 use(p, group * 4 + (z + d) % 4)
 
         def over_fin(p):
@@ -423,44 +431,44 @@
             for k in range(2):
                 own2[p, :, :, k * 512 : (k + 1) * 512] = columns(c, k)
 
-        def paired2(p, yy, half):
-            part = pl.ds(yy * 4 + half * 2, 2)
-            return own2[p, part] + cr2[p, part].astype(F32)
+        def paired2(p, n):
+            return own2[p, n] + cr2[p, n].astype(F32)
+
+        def beside2(p, g):
+            yy = (y + ORDER[g]) % 4
+            part = pl.ds(yy * 4, 4)
+            arrived(cr2.at[p, part], c2_r.at[p, g])
+            qs2[p, yy] = (own2[p, part] + cr2[p, part].astype(F32)).astype(BF)
+            to, dev = ((yfm2, dev_up), (yfp2, dev_down))[g]
+            send(qs2.at[p, yy], to.at[p], y2_s.at[p, g], y2_r.at[p, g], dev)
 
         def opposite2(p):
-            arrived(cr2.at[p, pl.ds(far * 4, 4)], c2_r.at[p, 0])
-            qs2[p, far, a] = paired2(p, far, 0).astype(BF)
-            send(qs2.at[p, far, a], ya2.at[p], y2_s.at[p, 0], y2_r.at[p, 0], dev_up)
-            qs2[p, far, b] = paired2(p, far, 1).astype(BF)
-            send(qs2.at[p, far, b], yb2.at[p], y2_s.at[p, 1], y2_r.at[p, 1], dev_down)
-
-        def beside2(p):
-            arrived(cr2.at[p, pl.ds(up * 4, 4)], c2_r.at[p, 1])
-            qs2[p, up, b] = paired2(p, up, 1).astype(BF)
-            send(qs2.at[p, up, b], yfm2.at[p, b], y2_s.at[p, 2], y2_r.at[p, 2], dev_up)
-            arrived(cr2.at[p, pl.ds(down * 4, 4)], c2_r.at[p, 2])
-            qs2[p, down, a] = paired2(p, down, 0).astype(BF)
-            send(qs2.at[p, down, a], yfp2.at[p, a], y2_s.at[p, 3], y2_r.at[p, 3], dev_down)
+            arrived(cr2.at[p, pl.ds(far * 4, 4)], c2_r.at[p, 2])
+            for d in (2, 1, 3):
+                zz = (z + d) % 4
+                qs2[p, far, zz] = paired2(p, far * 4 + (3 - zz)).astype(BF)
+                send(
+                    qs2.at[p, far, zz], zfar2.at[p, z], zf2_s.at[p, d], zf2_r.at[p, z],
+                    at(1, f, y, zz, c),
+                )
 
         def onward2(p):
-            arrived(ya2.at[p], y2_r.at[p, 0])
-            qs2[p, up, a] = (paired2(p, up, 0) + ya2[p].astype(F32)).astype(BF)
-            send(qs2.at[p, up, a], yfm2.at[p, a], y2_s.at[p, 4], y2_r.at[p, 4], dev_up)
-            arrived(yb2.at[p], y2_r.at[p, 1])
-            qs2[p, down, b] = (paired2(p, down, 1) + yb2[p].astype(F32)).astype(BF)
-            send(qs2.at[p, down, b], yfp2.at[p, b], y2_s.at[p, 5], y2_r.at[p, 5], dev_down)
+            value = paired2(p, far * 4 + zt)
+            for d in (1, 3, 2):
+                zz = (z + d) % 4
+                arrived(zfar2.at[p, zz], zf2_r.at[p, zz])
+                value = value + zfar2[p, zz].astype(F32)
+            fs2[p] = value.astype(BF)
+            send(fs2.at[p], ffar2.at[p], y2_s.at[p, 2], y2_r.at[p, 2], dev_far)
 
         def over_z2(p):
             part = pl.ds(y * 4, 4)
             arrived(cr2.at[p, part], c2_r.at[p, 3])
-            arrived(yfm2.at[p, b], y2_r.at[p, 2])
-            arrived(yfp2.at[p, a], y2_r.at[p, 3])
-            arrived(yfm2.at[p, a], y2_r.at[p, 4])
-            arrived(yfp2.at[p, b], y2_r.at[p, 5])
+            arrived(yfm2.at[p], y2_r.at[p, 0])
+            arrived(yfp2.at[p], y2_r.at[p, 1])
 
             def summed(k):
-                value = own2[p, y * 4 + k] + cr2[p, y * 4 + k].astype(F32)
-                return value + yfm2[p, k].astype(F32) + yfp2[p, k].astype(F32)
+                return paired2(p, y * 4 + k) + yfm2[p, k].astype(F32) + yfp2[p, k].astype(F32)
 
             for d in (2, 1, 3):
                 zz = (z + d) % 4
@@ -484,6 +492,8 @@
                 zz = (z + d) % 4
                 arrived(zin2.at[p, zz], z2_r.at[p, zz])
                 total = total + zin2[p, zz].astype(F32)
+            arrived(ffar2.at[p], y2_r.at[p, 2])
+            total = total + ffar2[p].astype(F32)
             for k in range(16):
                 rows = slice(k // 8 * 8, k // 8 * 8 + 8)
                 fo[:, k, :] = total[rows, k % 8 * 128 : (k % 8 + 1) * 128]
@@ -496,20 +506,22 @@
                 )
 
         project(0, 0)
+        project(0, 1)
+        beside(0, 0)
+        project(0, 2)
+        beside(0, 1)
         project(1, 0)
         opposite(0)
-        project(0, 1)
+        project(1, 1)
+        beside(1, 0)
+        project(1, 2)
+        beside(1, 1)
+        project(0, 3)
         opposite(1)
-        project(0, 2)
-        project(1, 1)
-        beside(0)
-        project(1, 2)
-        project(0, 3)
-        beside(1)
         project(1, 3)
         onward(0)
+        over_z(0)
         onward(1)
-        over_z(0)
         over_z(1)
         near(0)
         near(1)
@@ -517,36 +529,44 @@
         weights[2].wait()
         forward(0)
         forward(1)
-        for d in range(4):
-            beside_arrived(0, d)
-            use(0, y * 4 + (z + d) % 4)
-        for d in range(4):
-            beside_arrived(1, d)
-            use(0, down * 4 + (z + d) % 4)
-            use(0, up * 4 + (z + d) % 4)
-        for d in range(4):
-            opposite_arrived(0, d)
-            use(1, y * 4 + (z + d) % 4)
-        use_all(0, far)
+        for p in range(2):
+            spread_opposite(p)
+            taken(p, up, 0)
+            taken(p, down, 0)
+        use_at(0, (y, 0), (y, 1), (y, 2), (y, 3), (up, 0), (down, 0), (far, 0))
+        for d in range(1, 4):
+            taken(0, up, d)
+            taken(0, down, d)
+            use_at(1, (y, d - 1))
+            if d > 1:
+                use_at(0, (up, d - 1), (down, d - 1))
+        for d in range(1, 4):
+            taken(0, far, d)
+        use_at(0, (up, 3), (down, 3), (far, 1), (far, 2), (far, 3))
         over_fin(0)
-        for d in range(4):
-            opposite_arrived(1, d)
-            use(1, down * 4 + (z + d) % 4)
-            use(1, up * 4 + (z + d) % 4)
-        use_all(1, far)
+        for d in range(1, 4):
+            taken(1, up, d)
+            taken(1, down, d)
+            use_at(1, ((y, 3), (up, 0), (down, 0))[d - 1])
+        use_at(1, (far, 0), (up, 1), (down, 1), (up, 2), (down, 2))
+        for d in range(1, 4):
+            taken(1, far, d)
+        use_at(1, (up, 3), (down, 3), (far, 1), (far, 2), (far, 3))
         over_fin(1)
         hide(0)
         hide(1)
         weights[3].wait()
         lower(0)
+        beside2(0, 0)
+        beside2(0, 1)
         opposite2(0)
-        beside2(0)
         lower(1)
+        beside2(1, 0)
+        beside2(1, 1)
         opposite2(1)
-        beside2(1)
         onward2(0)
+        over_z2(0)
         onward2(1)
-        over_z2(0)
         over_z2(1)
         finish(0)
         finish(1)
@@ -568,21 +588,21 @@
         v(256, 128), v(4, 256, 128), v(256, 512),
         v(4, 64, 128), v(256, 128, dtype=F32), v(128, 256, dtype=F32),
         v(2, 16, 64, 256, dtype=F32), v(2, 16, 64, 256), v(2, 16, 64, 256), v(2, 4, 4, 64, 256),
-        v(2, 2, 64, 256), v(2, 2, 64, 256), v(2, 4, 64, 256), v(2, 4, 64, 256),
+        v(2, 4, 64, 256), v(2, 64, 256), v(2, 64, 256), v(2, 4, 64, 256), v(2, 4, 64, 256),
         v(2, 4, 64, 256), v(2, 4, 64, 256), v(2, 64, 256, dtype=F32),
         v(2, 16, 2, 64, 256), v(2, 128, 512, dtype=F32), v(2, 128, 128, dtype=F32),
         v(2, 4, 32, 640), v(2, 4, 32, 640), v(2, 128, 256),
         v(2, 16, 16, 1024, dtype=F32), v(2, 16, 16, 1024), v(2, 16, 16, 1024),
-        v(2, 4, 4, 16, 1024), v(2, 2, 16, 1024), v(2, 2, 16, 1024),
+        v(2, 4, 4, 16, 1024), v(2, 4, 16, 1024), v(2, 16, 1024), v(2, 16, 1024),
         v(2, 4, 16, 1024), v(2, 4, 16, 1024), v(2, 4, 16, 1024), v(2, 4, 16, 1024),
         v(2, 16, 1024, dtype=F32), v(8, 16, 128, dtype=F32), v(2, 8, 16, 128), v(8, 2, 16, 128),
     ]
     counts = [
-        (2,), (4,), (4,), (), (), (16,), (16,), (4,), (4,), (4,), (4,),
-        (2, 4), (2, 4), (2, 6), (2, 6), (2, 4), (2, 4),
-        (2, 4), (2, 12), (2, 16), (2, 16), (2, 16),
-        (2, 4), (2, 4), (2, 4), (2, 4), (2, 4), (2, 4), (2, 6), (2, 6), (2, 4), (2, 4),
-        (2, 8), (8,),
+        (2,), (4,), (4,), (), (), (16,), (16,), (4,), (4,), (4, 4), (4, 4),
+        (2, 4), (2, 4), (2, 3), (2, 3), (2, 4), (2, 4), (2, 4), (2, 4),
+        (2, 8), (2, 9), (2, 16), (2, 16), (2, 16),
+        (2, 4), (2, 4), (2, 4), (2, 4), (2, 4), (2, 4), (2, 3), (2, 3), (2, 4), (2, 4),
+        (2, 4), (2, 4), (2, 8), (8,),
     ]
     scratch += [pltpu.SemaphoreType.DMA(k) for k in counts]
     vm, hbm = pl.BlockSpec(memory_space=pltpu.VMEM), pl.BlockSpec(memory_space=pl.ANY)

time: 96 us -> 90.3 us (0.941)
  Pallas kernels: 94.3 us -> 88.7 us
    pallas_call x1, Pallas kernels: 94.3 us -> 88.7 us  [moved(): pl.pallas_call(kernel, out_shape=jax.ShapeDtypeStruct((2, D), BF), in_spe...]
where the time goes in v3:
time: 90.3 us; the launch traced here: 90.2 us
  Pallas kernels  88.7 us (98%)
  local copies, waits for them, and re-layouts  1.52 us (2%)
    pallas_call x1, Pallas kernels, moved(): pl.pallas_call(kernel, out_shape=jax.ShapeDtypeStruct((2, D), BF), in_spe...  88.7 us

profile of v3, /device:TPU:1, one launch (start us, length us, event | category | flops | bytes accessed | tf_op | source)
XLA Modules:
  0.0 90.2 jit_solution(7649992345196239717)
XLA Ops:
  0.0 88.7 %shard_map.100 = bf16[2,16384]{1,0:T(2,128)(2,1)} custom-call(bf16[2,16384]{1,0:T(2,128)(2,1)} %q_hbm.1, bf16[2,2048]{1,0:T(2,128)(2,1)} %fresh_hbm.1, s32[2]{0:T(128)} %lens.1, bf16[2,256,2048]{2,1,0:T(8,128)(2,1)} %bitcast.6, bf16[2,16384]{1,0:T(2,128)(2,1)} %res_hbm.1, bf16[4096]{0:T(1024)(128)(2,1)} %gain_hbm.1, bf16[512,4096]{1,0:T(8,128)(2,1)} %bitcast.5, ...), custom_call_target="tpu_custom_call" | custom-call | tf_op jit(solution)/shard_map/pallas_call | solution.py:610
  88.7 1.5 %copy.12 = bf16[2,16384]{1,0:T(2,128)(2,1)} copy(bf16[2,16384]{1,0:T(2,128)(2,1)} %shard_map.100) | data formatting | bytes 131072

commit v4 on v3

--- a/solution.py
+++ b/solution.py
@@ -11,7 +11,7 @@
 BF = jnp.bfloat16
 F32 = jnp.float32
 MESH = pl.DeviceIdType.MESH
-ORDER = (1, 3, 2, 0)
+ORDER = (2, 1, 3, 0)
 
 
 def iota(shape, axis):
@@ -77,7 +77,7 @@
     q_hbm, fresh_hbm, lens, kv_hbm, res_hbm, gain_hbm, ow_hbm, gw_hbm, uw_hbm, dw_hbm, out,
     wide, wide_f, narrow, narrow_f, q, res_src, gain_in, gain, fin_f,
     kv, sco, m1s, m1, comb, m2s,
-    ow, gw, uw, dw, m2, m2all, lhs, rin, resid, acc,
+    ow, guw, dw, m2, m2all, lhs, rin, resid,
     own, cs, cr, qs, zfar, fs, ffar, yfm, yfp, zs, zin, tot,
     sbuf, gu, ss, xs, xr, hid,
     own2, cs2, cr2, qs2, zfar2, fs2, ffar2, yfm2, yfp2, zs2, zin2, tot2, fo, fb, fin_in,
@@ -96,13 +96,22 @@
     def at(s, ff, yy, zz, cc):
         return (s, ff, (yy * 4 + zz) * 2 + cc)
 
-    def send(src, dst, s_sem, r_sem, dev):
-        cp = pltpu.make_async_remote_copy(
+    def make(src, dst, s_sem, r_sem, dev):
+        return pltpu.make_async_remote_copy(
             src_ref=src, dst_ref=dst, send_sem=s_sem, recv_sem=r_sem,
             device_id=dev, device_id_type=MESH,
         )
+
+    def send(*what):
+        cp = make(*what)
         cp.start()
         copies.append(cp)
+
+    maybe = []
+
+    def send_if(cond, *what):
+        pl.when(cond)(lambda: make(*what).start())
+        maybe.append((cond, what))
 
     barrier = pltpu.get_barrier_semaphore()
 
@@ -189,7 +198,14 @@
             greet(at(1, d // 2, y, zt, d % 2))
         weights = [
             pltpu.make_async_copy(a, b, w_sem.at[k])
-            for k, (a, b) in enumerate(((ow_hbm, ow), (gw_hbm, gw), (uw_hbm, uw), (dw_hbm, dw)))
+            for k, (a, b) in enumerate(
+                (
+                    (ow_hbm, ow.at[pl.ds(0, 512)]),
+                    (gw_hbm, guw.at[:, pl.ds(0, 256)]),
+                    (uw_hbm, guw.at[:, pl.ds(256, 256)]),
+                    (dw_hbm, dw),
+                )
+            )
         ]
         for cp in weights:
             cp.start()
@@ -217,9 +233,23 @@
             lambda t: (t // 2) % 4 * 64 + ((t % 2) * 16 + (t // 8) % 16) * 2 + t // 128
         )
         resid[...] = jnp.dot(sel, rin[...].reshape(256, 128), preferred_element_type=F32)
+        eight = [
+            resid[half * 128 + n * 8 : half * 128 + n * 8 + 8, :] for n in range(16) for half in range(2)
+        ]
+        eight = jnp.concatenate(eight, axis=1)
+        ow[512:528, :] = jnp.concatenate([eight, jnp.zeros_like(eight)], axis=0).astype(BF)
+        ow[528:, :] = jnp.zeros((112, 4096), BF)
+        t = iota((256, 128), 0)
+        row_yz = ((t // 128 + c) % 2 * 64 + t % 64) // 8
+        here = (row_yz == yz) & (t // 64 % 2 == c) & (t % 8 == iota((256, 128), 1))
+        lhs[:, 512:] = here.astype(F32).astype(BF)
 
         pick = selection(
-            lambda t: (t // 8) % 16 * 16 + (t // 128) % 2 * 8 + t % 2 * 4 + t // 256, 1024
+            lambda t: ((t // 128 + c) % 2 * 8 + (t // 8) % 8) * 16
+            + (t // 64) % 2 * 8
+            + t % 2 * 4
+            + t // 256,
+            1024,
         )
         row_fin = (iota((1024, 128), 0) // 2) % 4
         for e in (0, 1, 3, 2):
@@ -248,41 +278,37 @@
             lhs[:, k * 128 : (k + 1) * 128] = picked[k * 256 : (k + 1) * 256, :].astype(BF)
         weights[0].wait()
 
-        def project(p, g):
-            mine = (c == p).astype(F32)
+        def project(g):
             yy = (y + ORDER[g]) % 4
 
-            def chunk(k, carry):
-                n = yy * 4 + k
-                w = ow[:, pl.ds(pl.multiple_of(n * 256, 256), 256)]
-                acc[...] = jnp.dot(
-                    lhs[p * 128 : (p + 1) * 128, :], w, preferred_element_type=F32
-                )
-                r8 = pl.ds(pl.multiple_of(yz * 8, 8), 8)
-                lo = resid[pl.ds(pl.multiple_of(n * 8, 8), 8), :]
-                hi = resid[pl.ds(pl.multiple_of(128 + n * 8, 8), 8), :]
-                acc[r8, :] = acc[r8, :] + jnp.concatenate([lo, hi], axis=1) * mine
-                own[p, n] = acc[pl.ds(pl.multiple_of(c * 64, 64), 64), :]
-                cs[p, n] = acc[pl.ds(pl.multiple_of(oc * 64, 64), 64), :].astype(BF)
-                return carry
-
-            lax.fori_loop(0, 4, chunk, 0)
+            w = ow[:, pl.ds(pl.multiple_of(yy * 1024, 1024), 1024)]
+            value = jnp.dot(lhs[...], w, preferred_element_type=F32)
+            for p in range(2):
+                for k in range(4):
+                    cols = slice(k * 256, (k + 1) * 256)
+                    cs[p, yy * 4 + k] = value[128 + p * 64 : 192 + p * 64, cols].astype(BF)
+                    own[p, yy * 4 + k] = value[p * 64 : p * 64 + 64, cols]
             part = pl.ds(yy * 4, 4)
-            send(cs.at[p, part], cr.at[p, part], c_s.at[p, g], c_r.at[p, g], dev_core)
+            for p in range(2):
+                send(cs.at[p, part], cr.at[p, part], c_s.at[p, g], c_r.at[p, g], dev_core)
 
         def paired(p, n):
             return own[p, n] + cr[p, n].astype(F32)
 
         def beside(p, g):
             yy = (y + ORDER[g]) % 4
-            part = pl.ds(yy * 4, 4)
-            arrived(cr.at[p, part], c_r.at[p, g])
-            qs[p, yy] = (own[p, part] + cr[p, part].astype(F32)).astype(BF)
-            to, dev = ((yfm, dev_up), (yfp, dev_down))[g]
-            send(qs.at[p, yy], to.at[p], y_s.at[p, g], y_r.at[p, g], dev)
+            arrived(cr.at[p, pl.ds(yy * 4, 4)], c_r.at[p, g])
+            to, dev = ((yfm, dev_up), (yfp, dev_down))[g - 1]
+            for d in (2, 1, 3, 0):
+                k = (z + d) % 4
+                qs[p, yy, k] = paired(p, yy * 4 + k).astype(BF)
+                send(
+                    qs.at[p, yy, k], to.at[p, k],
+                    y_s.at[p, (g - 1) * 4 + d], y_r.at[p, (g - 1) * 4 + k], dev,
+                )
 
         def opposite(p):
-            arrived(cr.at[p, pl.ds(far * 4, 4)], c_r.at[p, 2])
+            arrived(cr.at[p, pl.ds(far * 4, 4)], c_r.at[p, 0])
             for d in (2, 1, 3):
                 zz = (z + d) % 4
                 qs[p, far, zz] = paired(p, far * 4 + zz).astype(BF)
@@ -298,15 +324,15 @@
                 arrived(zfar.at[p, zz], zf_r.at[p, zz])
                 value = value + zfar[p, zz].astype(F32)
             fs[p] = value.astype(BF)
-            send(fs.at[p], ffar.at[p], y_s.at[p, 2], y_r.at[p, 2], dev_far)
+            send(fs.at[p], ffar.at[p], y_s.at[p, 8], y_r.at[p, 8], dev_far)
 
         def over_z(p):
             part = pl.ds(y * 4, 4)
             arrived(cr.at[p, part], c_r.at[p, 3])
-            arrived(yfm.at[p], y_r.at[p, 0])
-            arrived(yfp.at[p], y_r.at[p, 1])
 
             def summed(k):
+                arrived(yfm.at[p, k], y_r.at[p, k])
+                arrived(yfp.at[p, k], y_r.at[p, 4 + k])
                 return paired(p, y * 4 + k) + yfm[p, k].astype(F32) + yfp[p, k].astype(F32)
 
             for d in (2, 1, 3):
@@ -327,16 +353,18 @@
             ref = sbuf.at[p, n, c]
             send(ref, ref, ac_s.at[p, n], ac_r.at[p, n], dev_core)
 
-        def use(p, n):
-            arrived(sbuf.at[p, n, oc], ac_r.at[p, n])
-            x = sbuf[p, n].reshape(128, 256).astype(F32)
-            sq = x * x
-            ss[p] += sq[:, :128] + sq[:, 128:]
-            pair = [gain[pl.ds(n * 2 + k, 1), :] for k in range(2)]
-            xg = (x * jnp.concatenate(pair, axis=1)).astype(BF)
-            rows = pl.ds(pl.multiple_of(n * 256, 256), 256)
-            gu[p, :, :256] += jnp.dot(xg, gw[rows, :], preferred_element_type=F32)
-            gu[p, :, 256:] += jnp.dot(xg, uw[rows, :], preferred_element_type=F32)
+        def use(p, yy):
+            parts = []
+            for k in range(4):
+                n = yy * 4 + k
+                arrived(sbuf.at[p, n, oc], ac_r.at[p, n])
+                x = sbuf[p, n].reshape(128, 256).astype(F32)
+                sq = x * x
+                ss[p] += sq[:, :128] + sq[:, 128:]
+                pair = [gain[pl.ds(n * 2 + m, 1), :] for m in range(2)]
+                parts.append((x * jnp.concatenate(pair, axis=1)).astype(BF))
+            w = guw[pl.ds(pl.multiple_of(yy * 1024, 1024), 1024), :]
+            gu[p] += jnp.dot(jnp.concatenate(parts, axis=1), w, preferred_element_type=F32)
 
         def near(p):
             total = tot[p]
@@ -344,7 +372,7 @@
                 zz = (z + d) % 4
                 arrived(zin.at[p, zz], z_r.at[p, zz])
                 total = total + zin[p, zz].astype(F32)
-            arrived(ffar.at[p], y_r.at[p, 2])
+            arrived(ffar.at[p], y_r.at[p, 8])
             total = total + ffar[p].astype(F32)
             sbuf[p, yz, c] = total.astype(BF)
             for d in (2, 1, 3):
@@ -360,26 +388,28 @@
                 n = y * 4 + (z + d) % 4
                 arrived(sbuf.at[p, n, c], ag_r.at[p, n])
                 give_y(p, n, d)
+                if d != 2:
+                    ref = sbuf.at[p, n, c]
+                    last = z == (3 if d == 1 else 0)
+                    send_if(last, ref, ref, ay_s.at[p, 8 + d], ag_r.at[p, n], dev_far)
                 give_core(p, n)
 
         def spread_opposite(p):
             n = far * 4 + z
             arrived(sbuf.at[p, n, c], ag_r.at[p, n])
-            for d in (2, 1, 3):
-                ref = sbuf.at[p, n, c]
-                send(
-                    ref, ref, az_s.at[p, 4 + d], ag_r.at[p, n], at(1, f, y, (z + d) % 4, c)
-                )
+            ref = sbuf.at[p, n, c]
+            for d in (2, 1, 3):
+                what = (ref, ref, az_s.at[p, 4 + d], ag_r.at[p, n], at(1, f, y, (z + d) % 4, c))
+                if d == 2:
+                    send(*what)
+                else:
+                    send_if(z != (3 if d == 1 else 0), *what)
             give_core(p, n)
 
         def taken(p, group, d):
             n = group * 4 + (z + d) % 4
             arrived(sbuf.at[p, n, c], ag_r.at[p, n])
             give_core(p, n)
-
-        def use_at(p, *places):
-            for group, d in places:
-                use(p, group * 4 + (z + d) % 4)
 
         def over_fin(p):
             tt = jnp.sum(ss[p], axis=1, keepdims=True)
@@ -414,36 +444,38 @@
                 ref = hid.at[p, pl.ds(pl.multiple_of(ff * 32, 32), 32)]
                 arrived(ref, xh_r.at[p, ff])
 
-            def columns(core, k):
+            def columns(core):
                 parts = []
                 for half in range(2):
-                    start = core * 2048 + half * 1024 + k * 512
-                    w = dw[:, pl.ds(pl.multiple_of(start, 512), 512)]
+                    start = core * 2048 + half * 1024
+                    w = dw[:, pl.ds(pl.multiple_of(start, 1024), 1024)]
                     value = jnp.dot(hid[p], w, preferred_element_type=F32)
-                    parts.append(value.reshape(16, 8, 512))
+                    parts.append(value.reshape(16, 8, 1024))
                 return jnp.concatenate(parts, axis=1)
 
-            for k in range(2):
-                cs2[p, :, :, k * 512 : (k + 1) * 512] = columns(oc, k).astype(BF)
+            cs2[p] = columns(oc).astype(BF)
             for g in range(4):
                 part = pl.ds((y + ORDER[g]) % 4 * 4, 4)
                 send(cs2.at[p, part], cr2.at[p, part], c2_s.at[p, g], c2_r.at[p, g], dev_core)
-            for k in range(2):
-                own2[p, :, :, k * 512 : (k + 1) * 512] = columns(c, k)
+            own2[p] = columns(c)
 
         def paired2(p, n):
             return own2[p, n] + cr2[p, n].astype(F32)
 
         def beside2(p, g):
             yy = (y + ORDER[g]) % 4
-            part = pl.ds(yy * 4, 4)
-            arrived(cr2.at[p, part], c2_r.at[p, g])
-            qs2[p, yy] = (own2[p, part] + cr2[p, part].astype(F32)).astype(BF)
-            to, dev = ((yfm2, dev_up), (yfp2, dev_down))[g]
-            send(qs2.at[p, yy], to.at[p], y2_s.at[p, g], y2_r.at[p, g], dev)
+            arrived(cr2.at[p, pl.ds(yy * 4, 4)], c2_r.at[p, g])
+            to, dev = ((yfm2, dev_up), (yfp2, dev_down))[g - 1]
+            for d in (2, 1, 3, 0):
+                k = 3 - (z + d) % 4
+                qs2[p, yy, k] = paired2(p, yy * 4 + k).astype(BF)
+                send(
+                    qs2.at[p, yy, k], to.at[p, k],
+                    y2_s.at[p, (g - 1) * 4 + d], y2_r.at[p, (g - 1) * 4 + k], dev,
+                )
 
         def opposite2(p):
-            arrived(cr2.at[p, pl.ds(far * 4, 4)], c2_r.at[p, 2])
+            arrived(cr2.at[p, pl.ds(far * 4, 4)], c2_r.at[p, 0])
             for d in (2, 1, 3):
                 zz = (z + d) % 4
                 qs2[p, far, zz] = paired2(p, far * 4 + (3 - zz)).astype(BF)
@@ -459,15 +491,15 @@
                 arrived(zfar2.at[p, zz], zf2_r.at[p, zz])
                 value = value + zfar2[p, zz].astype(F32)
             fs2[p] = value.astype(BF)
-            send(fs2.at[p], ffar2.at[p], y2_s.at[p, 2], y2_r.at[p, 2], dev_far)
+            send(fs2.at[p], ffar2.at[p], y2_s.at[p, 8], y2_r.at[p, 8], dev_far)
 
         def over_z2(p):
             part = pl.ds(y * 4, 4)
             arrived(cr2.at[p, part], c2_r.at[p, 3])
-            arrived(yfm2.at[p], y2_r.at[p, 0])
-            arrived(yfp2.at[p], y2_r.at[p, 1])
 
             def summed(k):
+                arrived(yfm2.at[p, k], y2_r.at[p, k])
+                arrived(yfp2.at[p, k], y2_r.at[p, 4 + k])
                 return paired2(p, y * 4 + k) + yfm2[p, k].astype(F32) + yfp2[p, k].astype(F32)
 
             for d in (2, 1, 3):
@@ -492,7 +524,7 @@
                 zz = (z + d) % 4
                 arrived(zin2.at[p, zz], z2_r.at[p, zz])
                 total = total + zin2[p, zz].astype(F32)
-            arrived(ffar2.at[p], y2_r.at[p, 2])
+            arrived(ffar2.at[p], y2_r.at[p, 8])
             total = total + ffar2[p].astype(F32)
             for k in range(16):
                 rows = slice(k // 8 * 8, k // 8 * 8 + 8)
@@ -505,20 +537,16 @@
                     at(d % 2, ff, y, zt, p),
                 )
 
-        project(0, 0)
-        project(0, 1)
-        beside(0, 0)
-        project(0, 2)
+        project(0)
+        project(1)
+        opposite(0)
+        opposite(1)
         beside(0, 1)
-        project(1, 0)
-        opposite(0)
-        project(1, 1)
-        beside(1, 0)
-        project(1, 2)
+        project(2)
         beside(1, 1)
-        project(0, 3)
-        opposite(1)
-        project(1, 3)
+        beside(0, 2)
+        project(3)
+        beside(1, 2)
         onward(0)
         over_z(0)
         onward(1)
@@ -533,37 +561,37 @@
             spread_opposite(p)
             taken(p, up, 0)
             taken(p, down, 0)
-        use_at(0, (y, 0), (y, 1), (y, 2), (y, 3), (up, 0), (down, 0), (far, 0))
+        use(0, y)
+        use(1, y)
         for d in range(1, 4):
             taken(0, up, d)
             taken(0, down, d)
-            use_at(1, (y, d - 1))
-            if d > 1:
-                use_at(0, (up, d - 1), (down, d - 1))
         for d in range(1, 4):
             taken(0, far, d)
-        use_at(0, (up, 3), (down, 3), (far, 1), (far, 2), (far, 3))
-        over_fin(0)
+        use(0, up)
+        use(0, down)
         for d in range(1, 4):
             taken(1, up, d)
             taken(1, down, d)
-            use_at(1, ((y, 3), (up, 0), (down, 0))[d - 1])
-        use_at(1, (far, 0), (up, 1), (down, 1), (up, 2), (down, 2))
+        use(0, far)
+        over_fin(0)
         for d in range(1, 4):
             taken(1, far, d)
-        use_at(1, (up, 3), (down, 3), (far, 1), (far, 2), (far, 3))
+        use(1, up)
+        use(1, down)
+        use(1, far)
         over_fin(1)
         hide(0)
         hide(1)
         weights[3].wait()
         lower(0)
-        beside2(0, 0)
+        opposite2(0)
         beside2(0, 1)
-        opposite2(0)
+        beside2(0, 2)
         lower(1)
-        beside2(1, 0)
+        opposite2(1)
         beside2(1, 1)
-        opposite2(1)
+        beside2(1, 2)
         onward2(0)
         over_z2(0)
         onward2(1)
@@ -573,6 +601,8 @@
         deliver()
         for cp in copies:
             cp.wait_send()
+        for cond, what in maybe:
+            pl.when(cond)(lambda what=what: make(*what).wait_send())
 
 
 def moved(*args):
@@ -584,9 +614,9 @@
         v(4, 64, 128), v(4096), v(32, 128, dtype=F32), v(8, 2, 16, 128, dtype=F32),
         v(2, 256, 2048), v(256, 256, dtype=F32), v(128, 128), v(128, 128),
         v(16, 16, 128, dtype=F32), v(256, 128),
-        v(512, 4096), v(4096, 256), v(4096, 256), v(256, 4096),
-        v(256, 128), v(4, 256, 128), v(256, 512),
-        v(4, 64, 128), v(256, 128, dtype=F32), v(128, 256, dtype=F32),
+        v(640, 4096), v(4096, 512), v(256, 4096),
+        v(256, 128), v(4, 256, 128), v(256, 640),
+        v(4, 64, 128), v(256, 128, dtype=F32),
         v(2, 16, 64, 256, dtype=F32), v(2, 16, 64, 256), v(2, 16, 64, 256), v(2, 4, 4, 64, 256),
         v(2, 4, 64, 256), v(2, 64, 256), v(2, 64, 256), v(2, 4, 64, 256), v(2, 4, 64, 256),
         v(2, 4, 64, 256), v(2, 4, 64, 256), v(2, 64, 256, dtype=F32),
@@ -599,9 +629,9 @@
     ]
     counts = [
         (2,), (4,), (4,), (), (), (16,), (16,), (4,), (4,), (4, 4), (4, 4),
-        (2, 4), (2, 4), (2, 3), (2, 3), (2, 4), (2, 4), (2, 4), (2, 4),
-        (2, 8), (2, 9), (2, 16), (2, 16), (2, 16),
-        (2, 4), (2, 4), (2, 4), (2, 4), (2, 4), (2, 4), (2, 3), (2, 3), (2, 4), (2, 4),
+        (2, 4), (2, 4), (2, 9), (2, 9), (2, 4), (2, 4), (2, 4), (2, 4),
+        (2, 8), (2, 12), (2, 16), (2, 16), (2, 16),
+        (2, 4), (2, 4), (2, 4), (2, 4), (2, 4), (2, 4), (2, 9), (2, 9), (2, 4), (2, 4),
         (2, 4), (2, 4), (2, 8), (8,),
     ]
     scratch += [pltpu.SemaphoreType.DMA(k) for k in counts]

time: 90.3 us -> 85.1 us (0.942)
  Pallas kernels: 88.7 us -> 83.1 us
    pallas_call x1, Pallas kernels: 88.7 us -> 83.1 us  [moved(): pl.pallas_call(kernel, out_shape=jax.ShapeDtypeStruct((2, D), BF), in_spe...]
where the time goes in v4:
time: 85.1 us; the launch traced here: 84.6 us
  Pallas kernels  83.1 us (98%)
  local copies, waits for them, and re-layouts  1.52 us (2%)
    pallas_call x1, Pallas kernels, moved(): pl.pallas_call(kernel, out_shape=jax.ShapeDtypeStruct((2, D), BF), in_spe...  83.1 us

profile of v4, /device:TPU:1, one launch (start us, length us, event | category | flops | bytes accessed | tf_op | source)
XLA Modules:
  0.0 84.6 jit_solution(1854791837829275024)
XLA Ops:
  0.0 83.1 %shard_map.100 = bf16[2,16384]{1,0:T(2,128)(2,1)} custom-call(bf16[2,16384]{1,0:T(2,128)(2,1)} %q_hbm.1, bf16[2,2048]{1,0:T(2,128)(2,1)} %fresh_hbm.1, s32[2]{0:T(128)} %lens.1, bf16[2,256,2048]{2,1,0:T(8,128)(2,1)} %bitcast.6, bf16[2,16384]{1,0:T(2,128)(2,1)} %res_hbm.1, bf16[4096]{0:T(1024)(128)(2,1)} %gain_hbm.1, bf16[512,4096]{1,0:T(8,128)(2,1)} %bitcast.5, ...), custom_call_target="tpu_custom_call" | custom-call | tf_op jit(solution)/shard_map/pallas_call | solution.py:640
  83.1 1.5 %copy.12 = bf16[2,16384]{1,0:T(2,128)(2,1)} copy(bf16[2,16384]{1,0:T(2,128)(2,1)} %shard_map.100) | data formatting | bytes 131072

commit v5 on v4

--- a/solution.py
+++ b/solution.py
@@ -76,12 +76,12 @@
 def kernel(
     q_hbm, fresh_hbm, lens, kv_hbm, res_hbm, gain_hbm, ow_hbm, gw_hbm, uw_hbm, dw_hbm, out,
     wide, wide_f, narrow, narrow_f, q, res_src, gain_in, gain, fin_f,
-    kv, sco, m1s, m1, comb, m2s,
-    ow, guw, dw, m2, m2all, lhs, rin, resid,
+    kv, sco, m2s,
+    ow, guw, dw, m2, comb, m2o, m2all, lhs, rin, resid,
     own, cs, cr, qs, zfar, fs, ffar, yfm, yfp, zs, zin, tot,
     sbuf, gu, ss, xs, xr, hid,
     own2, cs2, cr2, qs2, zfar2, fs2, ffar2, yfm2, yfp2, zs2, zin2, tot2, fo, fb, fin_in,
-    in_sem, w_sem, kv_sem, m1_s, m1_r, m2_s, m2_r, rs_s, rs_r, xa_s, xa_r,
+    in_sem, w_sem, kv_sem, m2_s, m2_r, rs_s, rs_r, xa_s, xa_r,
     c_s, c_r, y_s, y_r, z_s, z_r, zf_s, zf_r, az_s, ay_s, ac_s, ag_r, ac_r,
     xs_s, xs_r, xh_s, xh_r, c2_s, c2_r, y2_s, y2_r, z2_s, z2_r, zf2_s, zf2_r, f_s, f_r,
 ):
@@ -91,6 +91,8 @@
     oc = 1 - c
     j = f * 2 + c
     zt = 3 - z
+    along_z = (z, z + 1 - 2 * (z % 2), (z + 2) % 4, 3 - z)
+    at_end = z % 3 == 0
     copies = []
 
     def at(s, ff, yy, zz, cc):
@@ -121,9 +123,9 @@
     def deliver():
         for s in range(8):
             arrived(fin_in.at[s], f_r.at[s])
-        fin_f[...] = fin_in[...].astype(F32)
-        parts = [fin_f[s, :, k, :] for s in range(8) for k in range(16)]
-        out[...] = jnp.concatenate(parts, axis=1).astype(BF)
+            fin_f[s] = fin_in[s].astype(F32)
+            parts = [fin_f[s, :, k, :] for k in range(16)]
+            out[:, s * 2048 : (s + 1) * 2048] = jnp.concatenate(parts, axis=1).astype(BF)
 
     @pl.when(side == 0)
     def _attention_side():
@@ -138,7 +140,6 @@
         second_in = pltpu.make_async_copy(fresh_hbm, narrow, in_sem.at[1])
         first_in.start()
         second_in.start()
-        greet(at(0, f, y, z, oc))
         for d in range(8):
             greet(at(1, d // 2, y, zt, d % 2))
         first_in.wait()
@@ -153,16 +154,10 @@
         fresh = narrow_f[...].reshape(32, 128)
         mixed = attend(q, fresh, lens, kv, kv_copies, sco)
         sel = selection(
-            lambda t: (t // 4) % 2 * 128 + (t // 8) % 16 * 8 + (t // 128 + c) % 2 * 4 + t % 4
+            lambda t: (t // 4) % 2 * 128 + t // 16 * 8 + (t // 8) % 2 * 4 + t % 4
         )
-        moved_rows = jnp.dot(sel, mixed, preferred_element_type=F32)
-        m1s[...] = moved_rows[128:, :].astype(BF)
-        comb[:, pl.ds(pl.multiple_of(c * 8, 8), 8), :] = moved_rows[:128, :].reshape(16, 8, 128)
-        pl.semaphore_wait(barrier, 17)
-        send(m1s, m1, m1_s, m1_r, at(0, f, y, z, oc))
-        arrived(m1, m1_r)
-        comb[:, pl.ds(pl.multiple_of(oc * 8, 8), 8), :] = m1[...].astype(F32).reshape(16, 8, 128)
-        m2s[...] = comb[...].reshape(256, 128).astype(BF)
+        m2s[...] = jnp.dot(sel, mixed, preferred_element_type=F32).astype(BF)
+        pl.semaphore_wait(barrier, 16)
         for b in range(16):
             send(
                 m2s.at[pl.ds(b * 16, 16)],
@@ -189,7 +184,8 @@
             greet(at(0, f, d // 4, d % 4, c))
         for d in range(1, 4):
             greet(at(1, (f + d) % 4, y, z, c))
-            greet(at(1, f, y, (z + d) % 4, c))
+            greet(at(1, (f + d) % 4, y, z, oc))
+            greet(at(1, f, y, along_z[d], c))
         greet(dev_up)
         greet(dev_down)
         greet(dev_far)
@@ -220,7 +216,7 @@
             rows = wide_f[:, k * 32 : (k + 1) * 32, :]
             res_src[k] = rows.reshape(64, 128).astype(BF)
         gain[...] = gain_in[...].astype(F32).reshape(32, 128)
-        pl.semaphore_wait(barrier, 26)
+        pl.semaphore_wait(barrier, 29)
 
         for d in range(1, 4):
             ff = (f + d) % 4
@@ -245,8 +241,8 @@
         lhs[:, 512:] = here.astype(F32).astype(BF)
 
         pick = selection(
-            lambda t: ((t // 128 + c) % 2 * 8 + (t // 8) % 8) * 16
-            + (t // 64) % 2 * 8
+            lambda t: (t // 64) % 2 * 128
+            + ((t // 128 + c) % 2 * 8 + (t // 8) % 8) * 8
             + t % 2 * 4
             + t // 256,
             1024,
@@ -257,22 +253,36 @@
             for k in range(4):
                 n = yy * 4 + k
                 arrived(m2.at[pl.ds(pl.multiple_of(n * 16, 16), 16)], m2_r.at[n])
-            part = pl.ds(pl.multiple_of(yy * 64, 64), 64)
+            rows = pl.ds(pl.multiple_of(yy * 64, 64), 64)
+            part = pl.ds(pl.multiple_of(yy * 32, 32), 32)
+            comb[...] = m2[rows, :].astype(F32).reshape(4, 16, 128)
+            other = comb[:, pl.ds(pl.multiple_of(oc * 8, 8), 8), :]
+            m2o[part, :] = other.reshape(32, 128).astype(BF)
+            mine = comb[:, pl.ds(pl.multiple_of(c * 8, 8), 8), :]
+            m2all[f, c, part, :] = mine.reshape(32, 128).astype(BF)
             for d in (2, 1, 3):
                 ff = (f + d) % 4
-                send(
-                    m2.at[part], m2all.at[f, part], xa_s.at[d, e], xa_r.at[f, yy],
-                    at(1, ff, y, z, c),
-                )
+                to = m2all.at[f, c, part]
+                send(to, to, xa_s.at[d, e], xa_r.at[j, yy], at(1, ff, y, z, c))
+                send(m2o.at[part], to, xa_s.at[4 + d, e], xa_r.at[j, yy], at(1, ff, y, z, oc))
+            send(m2o.at[part], m2all.at[f, c, part], xa_s.at[0, e], xa_r.at[j, yy], dev_core)
+
+        def quarter(ff, cc):
+            for k in range(4):
+                arrived(m2all.at[ff, cc, pl.ds(k * 32, 32)], xa_r.at[ff * 2 + cc, k])
+
+        quarter(f, oc)
         picked = jnp.where(
-            row_fin == f, jnp.dot(pick, m2[...], preferred_element_type=F32), 0.0
+            row_fin == f, jnp.dot(pick, m2all[f].reshape(256, 128), preferred_element_type=F32), 0.0
         )
         for d in (1, 3, 2):
             ff = (f + d) % 4
-            for k in range(4):
-                arrived(m2all.at[ff, pl.ds(k * 64, 64)], xa_r.at[ff, k])
+            quarter(ff, c)
+            quarter(ff, oc)
             picked = jnp.where(
-                row_fin == ff, jnp.dot(pick, m2all[ff], preferred_element_type=F32), picked
+                row_fin == ff,
+                jnp.dot(pick, m2all[ff].reshape(256, 128), preferred_element_type=F32),
+                picked,
             )
         for k in range(4):
             lhs[:, k * 128 : (k + 1) * 128] = picked[k * 256 : (k + 1) * 256, :].astype(BF)
@@ -299,8 +309,8 @@
             yy = (y + ORDER[g]) % 4
             arrived(cr.at[p, pl.ds(yy * 4, 4)], c_r.at[p, g])
             to, dev = ((yfm, dev_up), (yfp, dev_down))[g - 1]
-            for d in (2, 1, 3, 0):
-                k = (z + d) % 4
+            for d in (3, 2, 1, 0):
+                k = along_z[d]
                 qs[p, yy, k] = paired(p, yy * 4 + k).astype(BF)
                 send(
                     qs.at[p, yy, k], to.at[p, k],
@@ -309,8 +319,8 @@
 
         def opposite(p):
             arrived(cr.at[p, pl.ds(far * 4, 4)], c_r.at[p, 0])
-            for d in (2, 1, 3):
-                zz = (z + d) % 4
+            for d in (3, 2, 1):
+                zz = along_z[d]
                 qs[p, far, zz] = paired(p, far * 4 + zz).astype(BF)
                 send(
                     qs.at[p, far, zz], zfar.at[p, z], zf_s.at[p, d], zf_r.at[p, z],
@@ -319,8 +329,8 @@
 
         def onward(p):
             value = paired(p, far * 4 + z)
-            for d in (1, 3, 2):
-                zz = (z + d) % 4
+            for d in (3, 2, 1):
+                zz = along_z[d]
                 arrived(zfar.at[p, zz], zf_r.at[p, zz])
                 value = value + zfar[p, zz].astype(F32)
             fs[p] = value.astype(BF)
@@ -335,8 +345,8 @@
                 arrived(yfp.at[p, k], y_r.at[p, 4 + k])
                 return paired(p, y * 4 + k) + yfm[p, k].astype(F32) + yfp[p, k].astype(F32)
 
-            for d in (2, 1, 3):
-                zz = (z + d) % 4
+            for d in (3, 2, 1):
+                zz = along_z[d]
                 zs[p, zz] = summed(zz).astype(BF)
                 send(zs.at[p, zz], zin.at[p, z], z_s.at[p, d], z_r.at[p, z], at(1, f, y, zz, c))
             tot[p] = summed(z)
@@ -368,46 +378,45 @@
 
         def near(p):
             total = tot[p]
-            for d in (1, 3, 2):
-                zz = (z + d) % 4
+            for d in (3, 2, 1):
+                zz = along_z[d]
                 arrived(zin.at[p, zz], z_r.at[p, zz])
                 total = total + zin[p, zz].astype(F32)
             arrived(ffar.at[p], y_r.at[p, 8])
             total = total + ffar[p].astype(F32)
             sbuf[p, yz, c] = total.astype(BF)
-            for d in (2, 1, 3):
-                zz = (z + d) % 4
+            give(p, yz, 8, dev_far)
+            for d in (3, 2, 1):
+                zz = along_z[d]
                 ref = sbuf.at[p, yz, c]
                 send(ref, ref, az_s.at[p, d], ag_r.at[p, yz], at(1, f, y, zz, c))
             give_y(p, yz, 0)
-            give(p, yz, 8, dev_far)
             give_core(p, yz)
 
         def forward(p):
-            for d in range(1, 4):
-                n = y * 4 + (z + d) % 4
+            for d in (3, 2, 1):
+                n = y * 4 + along_z[d]
                 arrived(sbuf.at[p, n, c], ag_r.at[p, n])
+                if d == 3:
+                    ref = sbuf.at[p, n, c]
+                    send_if(at_end, ref, ref, ay_s.at[p, 9], ag_r.at[p, n], dev_far)
                 give_y(p, n, d)
-                if d != 2:
-                    ref = sbuf.at[p, n, c]
-                    last = z == (3 if d == 1 else 0)
-                    send_if(last, ref, ref, ay_s.at[p, 8 + d], ag_r.at[p, n], dev_far)
                 give_core(p, n)
 
         def spread_opposite(p):
             n = far * 4 + z
             arrived(sbuf.at[p, n, c], ag_r.at[p, n])
             ref = sbuf.at[p, n, c]
-            for d in (2, 1, 3):
-                what = (ref, ref, az_s.at[p, 4 + d], ag_r.at[p, n], at(1, f, y, (z + d) % 4, c))
-                if d == 2:
+            for d in (3, 2, 1):
+                what = (ref, ref, az_s.at[p, 4 + d], ag_r.at[p, n], at(1, f, y, along_z[d], c))
+                if d == 3:
+                    send_if(z % 3 != 0, *what)
+                else:
                     send(*what)
-                else:
-                    send_if(z != (3 if d == 1 else 0), *what)
             give_core(p, n)
 
         def taken(p, group, d):
-            n = group * 4 + (z + d) % 4
+            n = group * 4 + along_z[d]
             arrived(sbuf.at[p, n, c], ag_r.at[p, n])
             give_core(p, n)
 
@@ -466,8 +475,8 @@
             yy = (y + ORDER[g]) % 4
             arrived(cr2.at[p, pl.ds(yy * 4, 4)], c2_r.at[p, g])
             to, dev = ((yfm2, dev_up), (yfp2, dev_down))[g - 1]
-            for d in (2, 1, 3, 0):
-                k = 3 - (z + d) % 4
+            for d in (3, 2, 1, 0):
+                k = 3 - along_z[d]
                 qs2[p, yy, k] = paired2(p, yy * 4 + k).astype(BF)
                 send(
                     qs2.at[p, yy, k], to.at[p, k],
@@ -476,8 +485,8 @@
 
         def opposite2(p):
             arrived(cr2.at[p, pl.ds(far * 4, 4)], c2_r.at[p, 0])
-            for d in (2, 1, 3):
-                zz = (z + d) % 4
+            for d in (3, 2, 1):
+                zz = along_z[d]
                 qs2[p, far, zz] = paired2(p, far * 4 + (3 - zz)).astype(BF)
                 send(
                     qs2.at[p, far, zz], zfar2.at[p, z], zf2_s.at[p, d], zf2_r.at[p, z],
@@ -486,8 +495,8 @@
 
         def onward2(p):
             value = paired2(p, far * 4 + zt)
-            for d in (1, 3, 2):
-                zz = (z + d) % 4
+            for d in (3, 2, 1):
+                zz = along_z[d]
                 arrived(zfar2.at[p, zz], zf2_r.at[p, zz])
                 value = value + zfar2[p, zz].astype(F32)
             fs2[p] = value.astype(BF)
@@ -502,8 +511,8 @@
                 arrived(yfp2.at[p, k], y2_r.at[p, 4 + k])
                 return paired2(p, y * 4 + k) + yfm2[p, k].astype(F32) + yfp2[p, k].astype(F32)
 
-            for d in (2, 1, 3):
-                zz = (z + d) % 4
+            for d in (3, 2, 1):
+                zz = along_z[d]
                 zs2[p, zz] = summed(3 - zz).astype(BF)
                 send(
                     zs2.at[p, zz], zin2.at[p, z], z2_s.at[p, d], z2_r.at[p, z], at(1, f, y, zz, c)
@@ -520,8 +529,8 @@
 
         def finish(p):
             total = tot2[p]
-            for d in (1, 3, 2):
-                zz = (z + d) % 4
+            for d in (3, 2, 1):
+                zz = along_z[d]
                 arrived(zin2.at[p, zz], z2_r.at[p, zz])
                 total = total + zin2[p, zz].astype(F32)
             arrived(ffar2.at[p], y2_r.at[p, 8])
@@ -563,23 +572,21 @@
             taken(p, down, 0)
         use(0, y)
         use(1, y)
-        for d in range(1, 4):
+        for d in (3, 2, 1):
             taken(0, up, d)
             taken(0, down, d)
-        for d in range(1, 4):
             taken(0, far, d)
         use(0, up)
         use(0, down)
-        for d in range(1, 4):
+        use(0, far)
+        over_fin(0)
+        for d in (3, 2, 1):
+            taken(1, far, d)
             taken(1, up, d)
             taken(1, down, d)
-        use(0, far)
-        over_fin(0)
-        for d in range(1, 4):
-            taken(1, far, d)
+        use(1, far)
         use(1, up)
         use(1, down)
-        use(1, far)
         over_fin(1)
         hide(0)
         hide(1)
@@ -612,10 +619,9 @@
     scratch = [
         v(2, D), v(2, 128, 128, dtype=F32), v(2, 2048), v(2, 16, 128, dtype=F32), v(256, 128),
         v(4, 64, 128), v(4096), v(32, 128, dtype=F32), v(8, 2, 16, 128, dtype=F32),
-        v(2, 256, 2048), v(256, 256, dtype=F32), v(128, 128), v(128, 128),
-        v(16, 16, 128, dtype=F32), v(256, 128),
+        v(2, 256, 2048), v(256, 256, dtype=F32), v(256, 128),
         v(640, 4096), v(4096, 512), v(256, 4096),
-        v(256, 128), v(4, 256, 128), v(256, 640),
+        v(256, 128), v(4, 16, 128, dtype=F32), v(128, 128), v(4, 2, 128, 128), v(256, 640),
         v(4, 64, 128), v(256, 128, dtype=F32),
         v(2, 16, 64, 256, dtype=F32), v(2, 16, 64, 256), v(2, 16, 64, 256), v(2, 4, 4, 64, 256),
         v(2, 4, 64, 256), v(2, 64, 256), v(2, 64, 256), v(2, 4, 64, 256), v(2, 4, 64, 256),
@@ -628,7 +634,7 @@
         v(2, 16, 1024, dtype=F32), v(8, 16, 128, dtype=F32), v(2, 8, 16, 128), v(8, 2, 16, 128),
     ]
     counts = [
-        (2,), (4,), (4,), (), (), (16,), (16,), (4,), (4,), (4, 4), (4, 4),
+        (2,), (4,), (4,), (16,), (16,), (4,), (4,), (8, 4), (8, 4),
         (2, 4), (2, 4), (2, 9), (2, 9), (2, 4), (2, 4), (2, 4), (2, 4),
         (2, 8), (2, 12), (2, 16), (2, 16), (2, 16),
         (2, 4), (2, 4), (2, 4), (2, 4), (2, 4), (2, 4), (2, 9), (2, 9), (2, 4), (2, 4),

time: 85.1 us -> 83.2 us (0.978)
  Pallas kernels: 83.1 us -> 81.5 us
    pallas_call x1, Pallas kernels: 83.1 us -> 81.5 us  [moved(): pl.pallas_call(kernel, out_shape=jax.ShapeDtypeStruct((2, D), BF), in_spe...]
where the time goes in v5:
time: 83.2 us; the launch traced here: 83 us
  Pallas kernels  81.5 us (98%)
  local copies, waits for them, and re-layouts  1.52 us (2%)
    pallas_call x1, Pallas kernels, moved(): pl.pallas_call(kernel, out_shape=jax.ShapeDtypeStruct((2, D), BF), in_spe...  81.5 us

profile of v5, /device:TPU:1, one launch (start us, length us, event | category | flops | bytes accessed | tf_op | source)
XLA Modules:
  0.0 83.0 jit_solution(8214271718158842432)
XLA Ops:
  0.0 81.5 %shard_map.100 = bf16[2,16384]{1,0:T(2,128)(2,1)} custom-call(bf16[2,16384]{1,0:T(2,128)(2,1)} %q_hbm.1, bf16[2,2048]{1,0:T(2,128)(2,1)} %fresh_hbm.1, s32[2]{0:T(128)} %lens.1, bf16[2,256,2048]{2,1,0:T(8,128)(2,1)} %bitcast.6, bf16[2,16384]{1,0:T(2,128)(2,1)} %res_hbm.1, bf16[4096]{0:T(1024)(128)(2,1)} %gain_hbm.1, bf16[512,4096]{1,0:T(8,128)(2,1)} %bitcast.5, ...), custom_call_target="tpu_custom_call" | custom-call | tf_op jit(solution)/shard_map/pallas_call | solution.py:646
  81.5 1.5 %copy.12 = bf16[2,16384]{1,0:T(2,128)(2,1)} copy(bf16[2,16384]{1,0:T(2,128)(2,1)} %shard_map.100) | data formatting | bytes 131072

commit v6 on v5

--- a/solution.py
+++ b/solution.py
@@ -78,9 +78,9 @@
     wide, wide_f, narrow, narrow_f, q, res_src, gain_in, gain, fin_f,
     kv, sco, m2s,
     ow, guw, dw, m2, comb, m2o, m2all, lhs, rin, resid,
-    own, cs, cr, qs, zfar, fs, ffar, yfm, yfp, zs, zin, tot,
+    own, cs, cr, qs, yd, sum1, zfar, fs, ffar, yfm, yfp, zs, zin, tot,
     sbuf, gu, ss, xs, xr, hid,
-    own2, cs2, cr2, qs2, zfar2, fs2, ffar2, yfm2, yfp2, zs2, zin2, tot2, fo, fb, fin_in,
+    own2, cs2, cr2, qs2, yd2, sum2, zfar2, fs2, ffar2, yfm2, yfp2, zs2, zin2, tot2, fo, fb, fin_in,
     in_sem, w_sem, kv_sem, m2_s, m2_r, rs_s, rs_r, xa_s, xa_r,
     c_s, c_r, y_s, y_r, z_s, z_r, zf_s, zf_r, az_s, ay_s, ac_s, ag_r, ac_r,
     xs_s, xs_r, xh_s, xh_r, c2_s, c2_r, y2_s, y2_r, z2_s, z2_r, zf2_s, zf2_r, f_s, f_r,
@@ -322,18 +322,32 @@
             for d in (3, 2, 1):
                 zz = along_z[d]
                 qs[p, far, zz] = paired(p, far * 4 + zz).astype(BF)
-                send(
+                what = (
                     qs.at[p, far, zz], zfar.at[p, z], zf_s.at[p, d], zf_r.at[p, z],
                     at(1, f, y, zz, c),
                 )
+                if d == 3:
+                    send_if(z % 3 != 0, *what)
+                    send_if(
+                        at_end, qs.at[p, far, zz], yd.at[p], y_s.at[p, 9], y_r.at[p, 9], dev_far
+                    )
+                else:
+                    send(*what)
 
         def onward(p):
             value = paired(p, far * 4 + z)
-            for d in (3, 2, 1):
+            for d in (2, 1):
                 zz = along_z[d]
                 arrived(zfar.at[p, zz], zf_r.at[p, zz])
                 value = value + zfar[p, zz].astype(F32)
-            fs[p] = value.astype(BF)
+            sum1[...] = value
+
+            @pl.when(z % 3 != 0)
+            def _from_third():
+                arrived(zfar.at[p, zt], zf_r.at[p, zt])
+                sum1[...] += zfar[p, zt].astype(F32)
+
+            fs[p] = sum1[...].astype(BF)
             send(fs.at[p], ffar.at[p], y_s.at[p, 8], y_r.at[p, 8], dev_far)
 
         def over_z(p):
@@ -347,7 +361,17 @@
 
             for d in (3, 2, 1):
                 zz = along_z[d]
-                zs[p, zz] = summed(zz).astype(BF)
+                value = summed(zz)
+                if d == 3:
+                    sum1[...] = value
+
+                    @pl.when(at_end)
+                    def _from_opposite():
+                        arrived(yd.at[p], y_r.at[p, 9])
+                        sum1[...] += yd[p].astype(F32)
+
+                    value = sum1[...]
+                zs[p, zz] = value.astype(BF)
                 send(zs.at[p, zz], zin.at[p, z], z_s.at[p, d], z_r.at[p, z], at(1, f, y, zz, c))
             tot[p] = summed(z)
 
@@ -488,18 +512,32 @@
             for d in (3, 2, 1):
                 zz = along_z[d]
                 qs2[p, far, zz] = paired2(p, far * 4 + (3 - zz)).astype(BF)
-                send(
+                what = (
                     qs2.at[p, far, zz], zfar2.at[p, z], zf2_s.at[p, d], zf2_r.at[p, z],
                     at(1, f, y, zz, c),
                 )
+                if d == 3:
+                    send_if(z % 3 != 0, *what)
+                    send_if(
+                        at_end, qs2.at[p, far, zz], yd2.at[p], y2_s.at[p, 9], y2_r.at[p, 9], dev_far
+                    )
+                else:
+                    send(*what)
 
         def onward2(p):
             value = paired2(p, far * 4 + zt)
-            for d in (3, 2, 1):
+            for d in (2, 1):
                 zz = along_z[d]
                 arrived(zfar2.at[p, zz], zf2_r.at[p, zz])
                 value = value + zfar2[p, zz].astype(F32)
-            fs2[p] = value.astype(BF)
+            sum2[...] = value
+
+            @pl.when(z % 3 != 0)
+            def _from_third():
+                arrived(zfar2.at[p, zt], zf2_r.at[p, zt])
+                sum2[...] += zfar2[p, zt].astype(F32)
+
+            fs2[p] = sum2[...].astype(BF)
             send(fs2.at[p], ffar2.at[p], y2_s.at[p, 8], y2_r.at[p, 8], dev_far)
 
         def over_z2(p):
@@ -513,7 +551,17 @@
 
             for d in (3, 2, 1):
                 zz = along_z[d]
-                zs2[p, zz] = summed(3 - zz).astype(BF)
+                value = summed(3 - zz)
+                if d == 3:
+                    sum2[...] = value
+
+                    @pl.when(at_end)
+                    def _from_opposite():
+                        arrived(yd2.at[p], y2_r.at[p, 9])
+                        sum2[...] += yd2[p].astype(F32)
+
+                    value = sum2[...]
+                zs2[p, zz] = value.astype(BF)
                 send(
                     zs2.at[p, zz], zin2.at[p, z], z2_s.at[p, d], z2_r.at[p, z], at(1, f, y, zz, c)
                 )
@@ -624,20 +672,22 @@
         v(256, 128), v(4, 16, 128, dtype=F32), v(128, 128), v(4, 2, 128, 128), v(256, 640),
         v(4, 64, 128), v(256, 128, dtype=F32),
         v(2, 16, 64, 256, dtype=F32), v(2, 16, 64, 256), v(2, 16, 64, 256), v(2, 4, 4, 64, 256),
+        v(2, 64, 256), v(64, 256, dtype=F32),
         v(2, 4, 64, 256), v(2, 64, 256), v(2, 64, 256), v(2, 4, 64, 256), v(2, 4, 64, 256),
         v(2, 4, 64, 256), v(2, 4, 64, 256), v(2, 64, 256, dtype=F32),
         v(2, 16, 2, 64, 256), v(2, 128, 512, dtype=F32), v(2, 128, 128, dtype=F32),
         v(2, 4, 32, 640), v(2, 4, 32, 640), v(2, 128, 256),
         v(2, 16, 16, 1024, dtype=F32), v(2, 16, 16, 1024), v(2, 16, 16, 1024),
-        v(2, 4, 4, 16, 1024), v(2, 4, 16, 1024), v(2, 16, 1024), v(2, 16, 1024),
+        v(2, 4, 4, 16, 1024), v(2, 16, 1024), v(16, 1024, dtype=F32),
+        v(2, 4, 16, 1024), v(2, 16, 1024), v(2, 16, 1024),
         v(2, 4, 16, 1024), v(2, 4, 16, 1024), v(2, 4, 16, 1024), v(2, 4, 16, 1024),
         v(2, 16, 1024, dtype=F32), v(8, 16, 128, dtype=F32), v(2, 8, 16, 128), v(8, 2, 16, 128),
     ]
     counts = [
         (2,), (4,), (4,), (16,), (16,), (4,), (4,), (8, 4), (8, 4),
-        (2, 4), (2, 4), (2, 9), (2, 9), (2, 4), (2, 4), (2, 4), (2, 4),
+        (2, 4), (2, 4), (2, 10), (2, 10), (2, 4), (2, 4), (2, 4), (2, 4),
         (2, 8), (2, 12), (2, 16), (2, 16), (2, 16),
-        (2, 4), (2, 4), (2, 4), (2, 4), (2, 4), (2, 4), (2, 9), (2, 9), (2, 4), (2, 4),
+        (2, 4), (2, 4), (2, 4), (2, 4), (2, 4), (2, 4), (2, 10), (2, 10), (2, 4), (2, 4),
         (2, 4), (2, 4), (2, 8), (8,),
     ]
     scratch += [pltpu.SemaphoreType.DMA(k) for k in counts]

time: 83.2 us -> 81.3 us (0.977)
  Pallas kernels: 81.5 us -> 79.6 us
    pallas_call x1, Pallas kernels: 81.5 us -> 79.6 us  [moved(): pl.pallas_call(kernel, out_shape=jax.ShapeDtypeStruct((2, D), BF), in_spe...]
where the time goes in v6:
time: 81.3 us; the launch traced here: 81.2 us
  Pallas kernels  79.6 us (98%)
  local copies, waits for them, and re-layouts  1.52 us (2%)
    pallas_call x1, Pallas kernels, moved(): pl.pallas_call(kernel, out_shape=jax.ShapeDtypeStruct((2, D), BF), in_spe...  79.6 us

profile of v6, /device:TPU:1, one launch (start us, length us, event | category | flops | bytes accessed | tf_op | source)
XLA Modules:
  0.0 81.2 jit_solution(855049146522849371)
XLA Ops:
  0.0 79.6 %shard_map.100 = bf16[2,16384]{1,0:T(2,128)(2,1)} custom-call(bf16[2,16384]{1,0:T(2,128)(2,1)} %q_hbm.1, bf16[2,2048]{1,0:T(2,128)(2,1)} %fresh_hbm.1, s32[2]{0:T(128)} %lens.1, bf16[2,256,2048]{2,1,0:T(8,128)(2,1)} %bitcast.6, bf16[2,16384]{1,0:T(2,128)(2,1)} %res_hbm.1, bf16[4096]{0:T(1024)(128)(2,1)} %gain_hbm.1, bf16[512,4096]{1,0:T(8,128)(2,1)} %bitcast.5, ...), custom_call_target="tpu_custom_call" | custom-call | tf_op jit(solution)/shard_map/pallas_call | solution.py:696
  79.6 1.5 %copy.12 = bf16[2,16384]{1,0:T(2,128)(2,1)} copy(bf16[2,16384]{1,0:T(2,128)(2,1)} %shard_map.100) | data formatting | bytes 131072

commit v7 on v6

--- a/solution.py
+++ b/solution.py
@@ -597,13 +597,13 @@
         project(0)
         project(1)
         opposite(0)
+        project(2)
+        beside(0, 1)
         opposite(1)
-        beside(0, 1)
-        project(2)
+        beside(0, 2)
         beside(1, 1)
-        beside(0, 2)
+        beside(1, 2)
         project(3)
-        beside(1, 2)
         onward(0)
         over_z(0)
         onward(1)
@@ -613,9 +613,10 @@
         weights[1].wait()
         weights[2].wait()
         forward(0)
+        spread_opposite(0)
+        spread_opposite(1)
         forward(1)
         for p in range(2):
-            spread_opposite(p)
             taken(p, up, 0)
             taken(p, down, 0)
         use(0, y)

time: 81.3 us -> 81.2 us (level); the launches traced: 81.2 us -> 80.2 us
  Pallas kernels: 79.6 us -> 78.7 us
    pallas_call x1, Pallas kernels: 79.6 us -> 78.7 us  [moved(): pl.pallas_call(kernel, out_shape=jax.ShapeDtypeStruct((2, D), BF), in_spe...]
where the time goes in v7:
time: 81.2 us; the launch traced here: 80.2 us
  Pallas kernels  78.7 us (97%)
  local copies, waits for them, and re-layouts  1.52 us (2%)
    pallas_call x1, Pallas kernels, moved(): pl.pallas_call(kernel, out_shape=jax.ShapeDtypeStruct((2, D), BF), in_spe...  78.7 us

profile of v7, /device:TPU:1, one launch (start us, length us, event | category | flops | bytes accessed | tf_op | source)
XLA Modules:
  0.0 80.2 jit_solution(15225112695307020296)
XLA Ops:
  0.0 78.7 %shard_map.100 = bf16[2,16384]{1,0:T(2,128)(2,1)} custom-call(bf16[2,16384]{1,0:T(2,128)(2,1)} %q_hbm.1, bf16[2,2048]{1,0:T(2,128)(2,1)} %fresh_hbm.1, s32[2]{0:T(128)} %lens.1, bf16[2,256,2048]{2,1,0:T(8,128)(2,1)} %bitcast.6, bf16[2,16384]{1,0:T(2,128)(2,1)} %res_hbm.1, bf16[4096]{0:T(1024)(128)(2,1)} %gain_hbm.1, bf16[512,4096]{1,0:T(8,128)(2,1)} %bitcast.5, ...), custom_call_target="tpu_custom_call" | custom-call | tf_op jit(solution)/shard_map/pallas_call | solution.py:697
  78.7 1.5 %copy.12 = bf16[2,16384]{1,0:T(2,128)(2,1)} copy(bf16[2,16384]{1,0:T(2,128)(2,1)} %shard_map.100) | data formatting | bytes 131072
